TPU v7x, 512 devices: a whole 4x4x16 slice. The times are simulated.
512 devices in a mesh: dp: 64 (over x, z), mp: 8 (over y, core).
Axes of the slice: x: 4, y: 4, z: 16, core: 2. Of those that a mesh axis runs over, the one named last changes fastest.
Arguments:
- checkpoint: bfloat16 [65536, 8192], P('dp', 'mp')
- key_grads: bfloat16 [65536, 1024], P('dp', 'mp'), may hold values from -16 to 16
- key_weight: bfloat16 [1024, 8192], P('dp', 'mp'), may hold values from -0.1875 to 0.1875
- norm_gain: float32 [8192], P('mp'), may hold values from 0.25 to 1.75
- picked_rows: int32 [64, 1024], P('dp'), may hold values from 0 to 1023, as said below
- row_counts: int32 [64], P('dp'), may hold values from 1 to 1024, as said below
Outputs:
- row_grads: bfloat16 [65536, 8192], P('dp', 'mp')
- weight_grad: float32 [1024, 8192], P('dp', 'mp')
- gain_grad: float32 [8192], P('mp')
Inputs may be any that keep to these rules, and one draw needn't show every extreme that they name: `picked_rows`: only the first row_counts[s] entries of row s are used; the entries of a row are distinct. `row_counts`: the counts sum to exactly 8192; one index of dp has exactly 1024, another exactly 1.
All inputs are finite; a program needn't handle non-finite values.
Results may differ from a plain program's by a relative error of at most 0.0029.
Values may be sent and summed in bfloat16 or wider, within the bound.
A program may use at most 64 MiB of HBM per device.

v0:
```python
import jax
import jax.numpy as jnp
from jax import lax
from jax.sharding import PartitionSpec as P

D = 8192


epsilon = 1e-05


def shards(checkpoint, key_grads, key_weight, norm_gain, picked_rows, row_counts):
    capacity = picked_rows.shape[1]
    row_ids = picked_rows[0]
    live = jnp.arange(capacity) < row_counts[0]
    chosen_x = jnp.where(
        live[:, None], jnp.take(checkpoint, row_ids, axis=0), jnp.zeros((), jnp.bfloat16)
    )
    chosen_g = jnp.where(
        live[:, None], jnp.take(key_grads, row_ids, axis=0), jnp.zeros((), jnp.bfloat16)
    )
    full_g = lax.all_gather(chosen_g, "mp", axis=1, tiled=True)
    rows_f = chosen_x.astype(jnp.float32)
    square = lax.psum(jnp.sum(rows_f * rows_f, axis=1), "mp")
    columns = full_g
    grad_hidden = jnp.dot(
        columns,
        lax.all_gather(key_weight, "dp", axis=0, tiled=True),
        preferred_element_type=jnp.float32,
    )
    scaled = norm_gain * grad_hidden
    inverse = lax.rsqrt(square / D + epsilon)
    normed = rows_f * inverse[:, None]
    inner = lax.psum(jnp.sum(scaled * normed, axis=1), "mp")
    grad_rows = (inverse[:, None] * (scaled - normed * (inner[:, None] / D))).astype(jnp.bfloat16)
    hidden_b = (normed * norm_gain).astype(jnp.bfloat16)
    columns = full_g
    weight_grad = lax.psum_scatter(
        jnp.dot(jnp.transpose(columns), hidden_b, preferred_element_type=jnp.float32),
        "dp",
        scatter_dimension=0,
        tiled=True,
    )
    gain_grad = lax.psum(jnp.sum(grad_hidden * normed, axis=0), "dp")
    home_rows = grad_rows
    home_rows = jnp.where(live[:, None], home_rows, jnp.zeros((), jnp.bfloat16))
    return (home_rows, weight_grad, gain_grad)


def solution(mesh):
    in_specs = (P("dp", "mp"), P("dp", "mp"), P("dp", "mp"), P("mp"), P("dp", None), P("dp"))
    out_specs = (P("dp", "mp"), P("dp", "mp"), P("mp"))
    return jax.shard_map(shards, mesh=mesh, in_specs=in_specs, out_specs=out_specs, check_vma=False)
```

profile of v0, /device:TPU:1, one launch (start us, length us, event | category | flops | bytes accessed | tf_op | source)
XLA Modules:
  0.0 895.9 jit_solution(3088104968195375777)
XLA Ops:
  7.2 0.0 copy-start
  7.2 0.0 all-gather.3.cloned.1.call-start
  8.0 0.7 compare_select_fusion
  8.7 0.7 iota_compare_fusion
  9.4 3.9 gather_fusion.1
  13.3 1.0 select_select_fusion.1
  14.3 0.0 all-gather.3.cloned.1.call-update
  14.3 0.0 all-gather.5.cloned.1.call-start
  14.4 0.7 all-gather.5.cloned.1.call-update
  15.1 0.0 reduce-scatter.2.cloned.1.call-start
  15.1 0.0 copy-done
  15.1 5.3 gather_fusion
  20.5 0.0 copy-start.1
  20.5 2.5 fusion.10
  23.0 18.7 %psum.21 = f32[1024]{0:T(1024)S(1)} all-reduce(f32[1024]{0:T(1024)S(1)} %fusion.10), channel_id=1, replica_groups=mesh['dp'=64,'mp'=8] {'mp'}, use_global_device_ids=true, to_apply=%region_1.2 | all-reduce | flops 1024 | bytes 8192 | tf_op jit(solution)/shard_map/psum | solution.py:24
  41.7 13.5 %all-gather.3.cloned.1.call-done = bf16[1024,1024]{1,0:T(8,128)(2,1)} async-done(((bf16[1024,128]{1,0:T(8,128)(2,1)}), bf16[1024,1024]{1,0:T(8,128)(2,1)}) %all-gather.3.cloned.1.call-update) | async-done | bytes 2097168 | tf_op jit(solution)/shard_map/all_gather | solution.py:22
  55.2 0.0 copy-done.1
  55.2 6.8 fusion.11
  62.0 0.0 reduce-scatter.2.cloned.1.call-update
  62.1 128.8 %all-gather.5.cloned.1.call-done = bf16[1024,1024]{1,0:T(8,128)(2,1)} async-done(((bf16[16,1024]{1,0:T(8,128)(2,1)}), bf16[1024,1024]{1,0:T(8,128)(2,1)}) %all-gather.5.cloned.1.call-update) | async-done | bytes 2097168 | tf_op jit(solution)/shard_map/all_gather | solution.py:28
  190.9 7.6 fusion.9
  198.5 113.8 %psum.23 = f32[1024]{0:T(1024)} all-reduce(f32[1024]{0:T(1024)S(1)} %get-tuple-element.3), channel_id=1, replica_groups=mesh['dp'=64,'mp'=8] {'dp'}, use_global_device_ids=true, to_apply=%region_6.7 | all-reduce | flops 1024 | bytes 8192 | tf_op jit(solution)/shard_map/psum | solution.py:44
  312.3 49.6 %psum.22 = f32[1024]{0:T(1024)S(1)} all-reduce(f32[1024]{0:T(1024)S(1)} %get-tuple-element.4), channel_id=1, replica_groups=mesh['dp'=64,'mp'=8] {'mp'}, use_global_device_ids=true, to_apply=%region_3.4 | all-reduce | flops 1024 | bytes 8192 | tf_op jit(solution)/shard_map/psum | solution.py:34
  361.9 4.6 fusion.13
  366.5 522.9 %reduce-scatter.2.cloned.1.call-done = f32[16,1024]{1,0:T(8,128)} async-done(((f32[1024,1024]{1,0:T(8,128)}), f32[16,1024]{1,0:T(8,128)}) %reduce-scatter.2.cloned.1.call-update) | async-done | bytes 65552 | tf_op jit(solution)/shard_map/reduce_scatter | solution.py:38
  (3 shorter events, 0.0 us)
Async XLA Ops:
  7.2 8.0 copy-start
  7.2 48.0 %all-gather.3.cloned.1.call-start = ((), (), s32[]{:S(2)}) async-start(), calls=%async_computation.1 | async-start | bytes 2359296 | tf_op jit(solution)/shard_map/all_gather | solution.py:22
  14.3 176.5 %all-gather.5.cloned.1.call-start = ((), (), s32[]{:S(2)}) async-start(), calls=%async_computation.2 | async-start | bytes 2129920 | tf_op jit(solution)/shard_map/all_gather | solution.py:28
  15.1 874.3 %reduce-scatter.2.cloned.1.call-start = ((), (), s32[]{:S(2)}) async-start(), calls=%async_computation.3 | async-start | bytes 4259840 | tf_op jit(solution)/shard_map/reduce_scatter | solution.py:38
  20.5 34.7 %copy-start.1 = (f32[1024]{0:T(1024)S(1)}, f32[1024]{0:T(1024)}, u32[]{:S(2)}) copy-start(f32[1024]{0:T(1024)} %param.9) | copy-start | bytes 12292
Sparse Core Ops, SparseCore 0:
  14.5 40.7 all-gather.2
  58.1 132.6 all-gather.4
  195.9 693.5 reduce-scatter.1
where the time goes:
time: 906 us; the launch traced here: 896 us
  waiting for transfers between devices  666 us (74%)
  blocking collectives  182 us (20%)
  between operations  14.6 us (2%)
  matrix products  14.5 us (2%)
  other arithmetic  9.55 us (1%)
  local copies, waits for them, and re-layouts  9.22 us (1%)
    reduce_scatter x1, waiting for transfers between devices, shards(): lax.psum_scatter(jnp.dot(jnp.transpose(columns), hidden_b, preferred_elem...  523 us
    all_gather x1, waiting for transfers between devices, shards(): lax.all_gather(key_weight, 'dp', axis=0, tiled=True)  129 us
    psum x1, blocking collectives, shards(): gain_grad = lax.psum(jnp.sum(grad_hidden * normed, axis=0), 'dp')  114 us
    psum x1, blocking collectives, shards(): inner = lax.psum(jnp.sum(scaled * normed, axis=1), 'mp')  49.6 us
    psum x1, blocking collectives, shards(): square = lax.psum(jnp.sum(rows_f * rows_f, axis=1), 'mp')  18.7 us
  transfers between devices with their start and end apart: 3, of which 3 were waited for; matrix products, arithmetic and copies ran while one was open for 3% of the time, Pallas kernels for 0%

commit v1 on v0

v1 whole, which is shorter than its diff:
```python
import functools

import jax
import jax.numpy as jnp
from jax import lax
from jax.experimental import pallas as pl
from jax.experimental.pallas import tpu as pltpu
from jax.sharding import PartitionSpec as P

D = 8192
EPS = 1e-05
NX, NZ, NY = 4, 16, 4
MESH = pl.DeviceIdType.MESH
F32, BF16 = jnp.float32, jnp.bfloat16
ORDER = (0, 3, 1, 2)


def rem(a, n):
    return lax.rem(a, n)


def dot(a, b):
    return jnp.dot(a, b, preferred_element_type=F32)


def kernel(
    x_in, kg_in, w_in, gain, picked, count,
    rows_out, wg_out, gg_out,
    X, KG, GT, W, H, GH, RG, OUT,
    inv_c,
    SQ, IN, GX, GZ,
    S2, D1, D3, F1, F3, U1, U3, R,
    RA, RB, DA, DB, SA, SB, ZM, ZP,
    lsem, osem, ws, wr, wxs, wxr, ys, yr, sqs, sqr, ins, inr, gxs, gxr, gzs, gzr,
    xs, xr, zs, zr,
):
    dp, mp = lax.axis_index("dp"), lax.axis_index("mp")
    x, z = lax.div(dp, NZ), rem(dp, NZ)
    y, c = lax.div(mp, 2), rem(mp, 2)
    pending = []

    def to_x(k):
        return (rem(x + k, NX) * NZ + z, mp)

    def to_z(k):
        return (x * NZ + rem(z + k, NZ), mp)

    def to_y(k):
        return (dp, rem(y + k, NY) * 2 + c)

    def to_mp(k):
        return (dp, rem(mp + k, 8))

    sibling = (dp, 2 * y + 1 - c)

    def send(src, dst, ss, rs, dev):
        copy = pltpu.make_async_remote_copy(
            src_ref=src, dst_ref=dst, send_sem=ss, recv_sem=rs, device_id=dev, device_id_type=MESH
        )
        copy.start()
        pending.append(copy)

    def arrived(dst, ss, rs, dev):
        pltpu.make_async_remote_copy(
            src_ref=dst, dst_ref=dst, send_sem=ss, recv_sem=rs, device_id=dev, device_id_type=MESH
        ).wait_recv()

    get_kg = pltpu.make_async_copy(kg_in, KG, lsem.at[0])
    get_x = pltpu.make_async_copy(x_in, X, lsem.at[1])
    get_w = pltpu.make_async_copy(w_in, W.at[x, z], lsem.at[2])
    get_kg.start()
    get_w.start()
    get_x.start()

    barrier = pltpu.get_barrier_semaphore()
    for k in range(1, 8):
        pl.semaphore_signal(barrier, inc=1, device_id=to_mp(k), device_id_type=MESH)
    for k in range(1, NX):
        pl.semaphore_signal(barrier, inc=1, device_id=to_x(k), device_id_type=MESH)
    for k in range(1, NZ):
        pl.semaphore_signal(barrier, inc=1, device_id=to_z(k), device_id_type=MESH)
    pl.semaphore_wait(barrier, 7 + NX - 1 + NZ - 1)

    get_w.wait()
    for k in range(1, NX):
        send(W.at[x, z], W.at[x, z], wxs.at[k], wxr.at[k], to_x(k))

    get_kg.wait()

    def flip(j, _):
        rows = pl.ds(pl.multiple_of(j * 128, 128), 128)
        GT[mp, :, rows] = KG[rows, :].T
        return 0

    lax.fori_loop(0, 8, flip, 0)

    def block(k, other=False):
        return rem(y + k, NY) * 2 + ((1 - c) if other else c)

    def half(b, h):
        return GT.at[b, pl.ds(64 * h, 64), :]

    send(half(mp, 0), half(mp, 0), ys.at[1], yr.at[1], to_y(1))
    send(half(mp, 1), half(mp, 1), ys.at[3], yr.at[3], to_y(3))
    send(half(mp, 1), half(mp, 1), ys.at[2], yr.at[2], to_y(1))
    send(half(mp, 0), half(mp, 0), ys.at[4], yr.at[4], to_y(3))
    send(GT.at[mp], GT.at[mp], ys.at[0], yr.at[0], sibling)

    eye = lax.broadcasted_iota(jnp.int32, (128, 128), 0) == lax.broadcasted_iota(
        jnp.int32, (128, 128), 1
    )

    def to_row(col):
        return jnp.sum(jnp.where(eye, col, 0.0), axis=0, keepdims=True)

    def to_col(row):
        return jnp.sum(jnp.where(eye, row, 0.0), axis=1, keepdims=True)

    get_x.wait()

    def squares(j, _):
        rows = X[pl.ds(pl.multiple_of(j * 128, 128), 128), :].astype(F32)
        SQ[mp, pl.ds(j, 1), :] = to_row(jnp.sum(rows * rows, axis=1, keepdims=True))
        return 0

    lax.fori_loop(0, 8, squares, 0)
    for k in range(1, 8):
        send(SQ.at[mp], SQ.at[mp], sqs.at[k], sqr.at[k], to_mp(k))

    live = lax.broadcasted_iota(jnp.int32, (1, 1024), 1) < count[0]
    wanted = jnp.where(live, picked[...], -1)

    def selected(j, _):
        number = lax.broadcasted_iota(jnp.int32, (128, 1024), 0) + j * 128
        hit = jnp.where(wanted == number, 1.0, 0.0)
        inv_c[pl.ds(pl.multiple_of(j * 128, 128), 128), :] = jnp.sum(hit, axis=1, keepdims=True)
        return 0

    lax.fori_loop(0, 8, selected, 0)

    def w_part(zz, h):
        return W.at[:, rem(zz + 2 * NZ, NZ), :, pl.ds(512 * h, 512)]

    def w_ways(s, h):
        return [d for d in (0, 1) if s < 7 or d == h]

    def w_arrive(s, h):
        for d in w_ways(s, h):
            zz = z - 1 - s if d == 0 else z + 1 + s
            part = w_part(zz, h)
            arrived(part, ws.at[s, h, d], wr.at[s, h, d], to_z(15 if d == 0 else 1))

    def w_step(s):
        for h in (0, 1):
            if s > 0:
                w_arrive(s - 1, h)
            for d in w_ways(s, h):
                part = w_part(z - s if d == 0 else z + s, h)
                send(part, part, ws.at[s, h, d], wr.at[s, h, d], to_z(1 if d == 0 else 15))

    for k in range(1, NX):
        part = W.at[rem(x + NX - k, NX), z]
        arrived(part, wxs.at[k], wxr.at[k], to_x(NX - k))
    w_step(0)

    for k in range(1, 8):
        arrived(SQ.at[rem(mp + 8 - k, 8)], sqs.at[k], sqr.at[k], to_mp(8 - k))
    total = SQ[0]
    for k in range(1, 8):
        total = total + SQ[k]
    SQ[8] = lax.rsqrt(total / D + EPS)

    def hidden(j, _):
        rows = pl.ds(pl.multiple_of(j * 128, 128), 128)
        inverse = to_col(SQ[8, pl.ds(j, 1), :]) * inv_c[rows, :]
        inv_c[rows, :] = inverse
        normed = X[rows, :].astype(F32) * inverse
        H[rows, :] = (normed * gain[...]).astype(BF16)
        return 0

    lax.fori_loop(0, 8, hidden, 0)

    arrived(half(block(3), 0), ys.at[1], yr.at[1], to_y(3))
    send(half(block(3), 0), half(block(3), 0), ys.at[5], yr.at[5], to_y(1))
    arrived(half(block(1), 1), ys.at[3], yr.at[3], to_y(1))
    send(half(block(1), 1), half(block(1), 1), ys.at[6], yr.at[6], to_y(3))
    w_step(1)
    arrived(half(block(3), 1), ys.at[2], yr.at[2], to_y(3))
    send(GT.at[block(3)], GT.at[block(3)], ys.at[7], yr.at[7], sibling)
    arrived(half(block(1), 0), ys.at[4], yr.at[4], to_y(1))
    send(GT.at[block(1)], GT.at[block(1)], ys.at[8], yr.at[8], sibling)
    w_step(2)
    arrived(half(block(2), 0), ys.at[5], yr.at[5], to_y(3))
    arrived(half(block(2), 1), ys.at[6], yr.at[6], to_y(1))
    send(GT.at[block(2)], GT.at[block(2)], ys.at[9], yr.at[9], sibling)
    w_step(3)
    arrived(GT.at[block(0, True)], ys.at[0], yr.at[0], sibling)
    arrived(GT.at[block(3, True)], ys.at[7], yr.at[7], sibling)
    arrived(GT.at[block(1, True)], ys.at[8], yr.at[8], sibling)
    arrived(GT.at[block(2, True)], ys.at[9], yr.at[9], sibling)

    def terms(k, left, right):
        b = rem(x + k, NX)

        def tile(n, _):
            lhs = GT[pl.ds(2 * b, 2)].reshape(256, 1024)
            here = pl.ds(pl.multiple_of(n * 256, 256), 256)
            low = dot(lhs, H[:, here])
            left[:, :, here] = low.reshape(16, 16, 256).astype(left.dtype)
            there = pl.ds(pl.multiple_of(n * 256 + 512, 256), 256)
            high = dot(lhs, H[:, there])
            right[:, :, here] = high.reshape(16, 16, 256).astype(right.dtype)
            return 0

        lax.fori_loop(0, 2, tile, 0)

    def group(ref, j):
        g = rem(lax.div(z, 4) + 2 + ORDER[j], 4)
        return ref.at[pl.ds(4 * g, 4)]

    def x_send(i, j, src, dst, d):
        send(group(src, j), group(dst, j), xs.at[i, j, d], xr.at[i, j, d], to_x(1 if d == 0 else 3))

    def x_arrived(i, j, dst, d):
        arrived(group(dst, j), xs.at[i, j, d], xr.at[i, j, d], to_x(3 if d == 0 else 1))

    terms(2, S2.at[0], S2.at[1])
    for j in range(4):
        x_send(0, j, S2.at[0], RA, 0)
        x_send(0, j, S2.at[1], RB, 1)
    terms(1, F1, D1)
    for j in range(4):
        x_send(1, j, D1, DB, 0)
    terms(3, D3, F3)
    for j in range(4):
        x_send(1, j, D3, DA, 1)
    terms(0, R.at[0], R.at[1])

    def relay(j):
        x_arrived(0, j, RA, 0)
        group(U1, j)[...] = (group(F1, j)[...] + group(RA, j)[...].astype(F32)).astype(BF16)
        x_send(2, j, U1, SA, 0)
        x_arrived(0, j, RB, 1)
        group(U3, j)[...] = (group(F3, j)[...] + group(RB, j)[...].astype(F32)).astype(BF16)
        x_send(2, j, U3, SB, 1)

    def owned(j):
        x_arrived(1, j, DB, 0)
        x_arrived(1, j, DA, 1)
        x_arrived(2, j, SA, 0)
        x_arrived(2, j, SB, 1)
        for h, (first, second) in enumerate(((DA, SA), (DB, SB))):
            mine = group(R.at[h], j)
            mine[...] = mine[...] + group(first, j)[...].astype(F32) + group(second, j)[...].astype(F32)

    for s in range(4, 8):
        w_step(s)
        relay(s - 4)

    def z_arrived(s, h, d):
        buf = (ZM if d == 0 else ZP).at[h, s]
        arrived(buf, zs.at[s, h, d], zr.at[s, h, d], to_z(1 if d == 0 else 15))

    def z_step(s):
        for h in (0, 1):
            for d in (0, 1) if s < 7 else (0,):
                buf = ZM if d == 0 else ZP
                owner = rem(z + 8 + s if d == 0 else z + 16 + 7 - s, NZ)
                if s == 0:
                    src = R.at[h, owner]
                else:
                    z_arrived(s - 1, h, d)
                    src = buf.at[h, s - 1]
                    src[...] = src[...] + R[h, owner]
                send(src, buf.at[h, s], zs.at[s, h, d], zr.at[s, h, d], to_z(15 if d == 0 else 1))

    def backward(r):
        rows = pl.ds(256 * r, 256)
        lhs = GT[:, :, rows].reshape(1024, 256).T

        def tile(n, _):
            here = pl.ds(pl.multiple_of(n * 256, 256), 256)
            GH[rows, here] = dot(lhs, W[:, :, :, here].reshape(1024, 256))
            return 0

        lax.fori_loop(0, 4, tile, 0)
        for i in (0, 1):
            j = 2 * r + i
            part = pl.ds(128 * j, 128)
            normed = X[part, :].astype(F32) * inv_c[part, :]
            product = GH[part, :] * normed
            sums = jnp.sum(product, axis=0, keepdims=True)
            for b in range(8):
                piece = sums[:, 128 * b : 128 * b + 128]
                if j == 0:
                    GX[x, b : b + 1, :] = piece
                else:
                    GX[x, b : b + 1, :] = GX[x, b : b + 1, :] + piece
            inner = jnp.sum(gain[...] * product, axis=1, keepdims=True)
            IN[mp, j : j + 1, :] = to_row(inner)

    for h in (0, 1):
        w_arrive(7, h)
    owned(0)
    owned(1)
    z_step(0)
    backward(0)
    owned(2)
    z_step(1)
    backward(1)
    z_step(2)
    backward(2)
    z_step(3)
    backward(3)
    for k in range(1, 8):
        send(IN.at[mp], IN.at[mp], ins.at[k], inr.at[k], to_mp(k))
    for k in range(1, NX):
        send(GX.at[x], GX.at[x], gxs.at[k], gxr.at[k], to_x(k))
    owned(3)
    z_step(4)
    for k in range(1, 8):
        arrived(IN.at[rem(mp + 8 - k, 8)], ins.at[k], inr.at[k], to_mp(8 - k))
    total = IN[0]
    for k in range(1, 8):
        total = total + IN[k]
    IN[8] = total / D
    for k in range(1, NX):
        arrived(GX.at[rem(x + NX - k, NX)], gxs.at[k], gxr.at[k], to_x(NX - k))
    GZ[z] = GX[0] + GX[1] + GX[2] + GX[3]
    for k in range(1, NZ):
        send(GZ.at[z], GZ.at[z], gzs.at[k], gzr.at[k], to_z(k))

    def finish(j, _):
        rows = pl.ds(pl.multiple_of(j * 128, 128), 128)
        inner = to_col(IN[8, pl.ds(j, 1), :])
        inverse = inv_c[rows, :]
        normed = X[rows, :].astype(F32) * inverse
        RG[rows, :] = (inverse * (gain[...] * GH[rows, :] - normed * inner)).astype(BF16)
        return 0

    lax.fori_loop(0, 8, finish, 0)
    z_step(5)

    def place(r):
        def column(i):
            row = picked[:, 256 * r + 128 * i : 256 * r + 128 * i + 128].astype(F32)
            return to_col(row)

        ids = jnp.concatenate([column(0), column(1)], axis=0).astype(jnp.int32)
        slot = lax.broadcasted_iota(jnp.int32, (256, 1), 0) + 256 * r
        ids = jnp.where(slot < count[0], ids, -1)
        number = lax.broadcasted_iota(jnp.int32, (256, 1024), 1)
        choice = jnp.where(ids == number, 1.0, 0.0).astype(BF16)
        rows = pl.ds(256 * r, 256)

        def tile(n, _):
            here = pl.ds(pl.multiple_of(n * 256, 256), 256)
            OUT[rows, here] = dot(choice, RG[:, here]).astype(BF16)
            return 0

        lax.fori_loop(0, 4, tile, 0)
        copy = pltpu.make_async_copy(OUT.at[rows], rows_out.at[rows], osem.at[r])
        copy.start()
        return copy

    written = [place(0), place(1)]
    z_step(6)
    written += [place(2), place(3)]
    z_step(7)
    for k in range(1, NZ):
        arrived(GZ.at[rem(z + NZ - k, NZ)], gzs.at[k], gzr.at[k], to_z(NZ - k))
    total = GZ[0]
    for k in range(1, NZ):
        total = total + GZ[k]
    gg_out[...] = total
    for h in (0, 1):
        z_arrived(7, h, 0)
        z_arrived(6, h, 1)
        wg_out[:, 512 * h : 512 * h + 512] = R[h, z] + ZM[h, 7] + ZP[h, 6]
    for copy in written:
        copy.wait()
    for copy in pending:
        copy.wait_send()


def shards(checkpoint, key_grads, key_weight, norm_gain, picked_rows, row_counts):
    any_space = pl.BlockSpec(memory_space=pl.ANY)
    vmem = pl.BlockSpec(memory_space=pltpu.VMEM)
    smem = pl.BlockSpec(memory_space=pltpu.SMEM)
    dma = pltpu.SemaphoreType.DMA
    halfblock = (16, 16, 512)
    scratch = [
        pltpu.VMEM((1024, 1024), BF16),
        pltpu.VMEM((1024, 128), BF16),
        pltpu.VMEM((8, 128, 1024), BF16),
        pltpu.VMEM((NX, NZ, 16, 1024), BF16),
        pltpu.VMEM((1024, 1024), BF16),
        pltpu.VMEM((1024, 1024), F32),
        pltpu.VMEM((1024, 1024), BF16),
        pltpu.VMEM((1024, 1024), BF16),
        pltpu.VMEM((1024, 1), F32),
        pltpu.VMEM((9, 8, 128), F32),
        pltpu.VMEM((9, 8, 128), F32),
        pltpu.VMEM((NX, 8, 128), F32),
        pltpu.VMEM((NZ, 8, 128), F32),
        pltpu.VMEM((2,) + halfblock, BF16),
        pltpu.VMEM(halfblock, BF16),
        pltpu.VMEM(halfblock, BF16),
        pltpu.VMEM(halfblock, F32),
        pltpu.VMEM(halfblock, F32),
        pltpu.VMEM(halfblock, BF16),
        pltpu.VMEM(halfblock, BF16),
        pltpu.VMEM((2,) + halfblock, F32),
        *[pltpu.VMEM(halfblock, BF16) for _ in range(6)],
        pltpu.VMEM((2, 8, 16, 512), F32),
        pltpu.VMEM((2, 7, 16, 512), F32),
        dma((3,)), dma((4,)),
        dma((8, 2, 2)), dma((8, 2, 2)),
        dma((NX,)), dma((NX,)),
        dma((10,)), dma((10,)),
        dma((8,)), dma((8,)),
        dma((8,)), dma((8,)),
        dma((NX,)), dma((NX,)),
        dma((NZ,)), dma((NZ,)),
        dma((3, 4, 2)), dma((3, 4, 2)),
        dma((8, 2, 2)), dma((8, 2, 2)),
    ]
    row_grads, weight_grad, gain_grad = pl.pallas_call(
        kernel,
        out_shape=(
            jax.ShapeDtypeStruct((1024, 1024), BF16),
            jax.ShapeDtypeStruct((16, 1024), F32),
            jax.ShapeDtypeStruct((8, 128), F32),
        ),
        in_specs=[any_space, any_space, any_space, vmem, vmem, smem],
        out_specs=(any_space, vmem, vmem),
        scratch_shapes=scratch,
        compiler_params=pltpu.CompilerParams(
            collective_id=0, has_side_effects=True, vmem_limit_bytes=48 * 1024 * 1024
        ),
        cost_estimate=pl.CostEstimate(flops=6 * 1024**3, bytes_accessed=8 * 1024**2, transcendentals=1024),
        name="norm_key_backward",
    )(checkpoint, key_grads, key_weight, norm_gain.reshape(1, 1024), picked_rows, row_counts)
    return row_grads, weight_grad, gain_grad.reshape(1024)


def solution(mesh):
    in_specs = (P("dp", "mp"), P("dp", "mp"), P("dp", "mp"), P("mp"), P("dp", None), P("dp"))
    out_specs = (P("dp", "mp"), P("dp", "mp"), P("mp"))
    return jax.shard_map(shards, mesh=mesh, in_specs=in_specs, out_specs=out_specs, check_vma=False)
```

time: 906 us -> 98.5 us (0.11); the launches traced: 896 us -> 98.1 us
  waiting for transfers between devices: 666 us -> 0 us
  blocking collectives: 182 us -> 0 us
  Pallas kernels: 0 us -> 89.6 us
  matrix products: 14.5 us -> 0 us
  between operations: 14.6 us -> 1.3 us
  other arithmetic: 9.55 us -> 0 us
    reduce_scatter x1 -> x0, waiting for transfers between devices: 523 us -> none  [shards(): lax.psum_scatter(jnp.dot(jnp.transpose(columns), hidden_b, preferred_elem...]
    psum x3 -> x0, blocking collectives: 182 us -> none  [the longest x1 114 us: shards(): gain_grad = lax.psum(jnp.sum(grad_hidden * normed, axis=0), 'dp')]
    all_gather x2 -> x0, waiting for transfers between devices: 142 us -> none  [the longest x1 129 us: shards(): lax.all_gather(key_weight, 'dp', axis=0, tiled=True)]
    pallas_call x0 -> x1, Pallas kernels: none -> 89.6 us  [shards(): pl.pallas_call(kernel, out_shape=(jax.ShapeDtypeStruct((1024, 1024), BF16...]
    dot_general x2 -> x0, matrix products: 14.5 us -> none  [the longest x1 7.64 us: shards(): jnp.dot(columns, lax.all_gather(key_weight, 'dp', axis=0, tiled=True), pr...]
    gather x2 -> x0, local copies, waits for them, and re-layouts: 9.2 us -> none  [the longest x1 5.34 us: shards(): jnp.take(checkpoint, row_ids, axis=0)]
  transfers between devices with their start and end apart: 3 -> 0, of which waited for: 3 -> 0; matrix products, arithmetic and copies ran while one was open for 3% -> 0% of each run, Pallas kernels for 0% -> 0%
where the time goes in v1:
time: 98.5 us; the launch traced here: 98.1 us
  Pallas kernels  89.6 us (91%)
  local copies, waits for them, and re-layouts  7.21 us (7%)
  between operations  1.3 us (1%)
    pallas_call x1, Pallas kernels, shards(): pl.pallas_call(kernel, out_shape=(jax.ShapeDtypeStruct((1024, 1024), BF16...  89.6 us
    unnamed x13, local copies, waits for them, and re-layouts  7.21 us

profile of v1, /device:TPU:1, one launch (start us, length us, event | category | flops | bytes accessed | tf_op | source)
XLA Modules:
  0.0 98.1 jit_solution(17503664708016899701)
XLA Ops:
  1.3 0.0 copy-start
  1.3 1.6 %copy-done = bf16[1024,1024]{1,0:T(8,128)(2,1)S(1)} copy-done((bf16[1024,1024]{1,0:T(8,128)(2,1)S(1)}, bf16[1024,1024]{1,0:T(8,128)(2,1)}, u32[]{:S(2)}) %copy-start) | copy-done | bytes 2097176
  2.9 0.0 copy-start.1
  2.9 0.9 copy-done.1
  3.8 0.0 copy-start.2
  3.8 0.8 copy-done.2
  4.6 0.0 copy-start.3
  4.6 0.7 copy-done.3
  5.3 0.0 copy-start.4
  5.3 0.7 copy-done.4
  6.0 89.6 %norm_key_backward.1 = (bf16[1024,1024]{1,0:T(8,128)(2,1)S(1)}, f32[16,1024]{1,0:T(8,128)S(1)}, f32[8,128]{1,0:T(8,128)S(1)}) custom-call(bf16[1024,1024]{1,0:T(8,128)(2,1)S(1)} %copy-done, bf16[1024,128]{1,0:T(8,128)(2,1)S(1)} %copy-done.1, bf16[16,1024]{1,0:T(8,128)(2,1)S(1)} %copy-done.2, f32[1,1024]{1,0:T(1,128)S(1)} %bitcast.3, ...), custom_call_target="tpu_custom_call" | custom-call | flops 6442450944 | bytes 8388608 | tf_op jit(solution)/shard_map/norm_key_backward/pallas_call | solution.py:428
  95.5 1.3 %copy.13 = bf16[1024,1024]{1,0:T(8,128)(2,1)} copy(bf16[1024,1024]{1,0:T(8,128)(2,1)S(1)} %get-tuple-element.12) | data formatting | bytes 4194304
  96.9 0.6 copy.14
  97.5 0.6 copy.15
Async XLA Ops:
  1.3 1.6 %copy-start = (bf16[1024,1024]{1,0:T(8,128)(2,1)S(1)}, bf16[1024,1024]{1,0:T(8,128)(2,1)}, u32[]{:S(2)}) copy-start(bf16[1024,1024]{1,0:T(8,128)(2,1)} %x_in.1) | copy-start | bytes 6291460
  2.9 0.9 copy-start.1
  3.8 0.8 copy-start.2
  4.6 0.7 copy-start.3
  5.3 0.7 copy-start.4

commit v2 on v1

v2 whole, which is shorter than its diff:
```python
import functools

import jax
import jax.numpy as jnp
from jax import lax
from jax.experimental import pallas as pl
from jax.experimental.pallas import tpu as pltpu
from jax.sharding import PartitionSpec as P

D = 8192
EPS = 1e-05
NX, NZ, NY = 4, 16, 4
MESH = pl.DeviceIdType.MESH
F32, BF16 = jnp.float32, jnp.bfloat16


def rem(a, n):
    return lax.rem(a, n)


def dot(a, b):
    return jnp.dot(a, b, preferred_element_type=F32)


def kernel(
    x_in, kg_in, w_in, gain_in, picked_in, count,
    rows_out, wg_out, gg_out,
    X, KG, GT, G, WR, W, H, GH, RG, OUT,
    gain, picked, inv_c,
    SQ, IN, GX, GZ,
    S2, D1, D3, F1, F3, U1, U3, R,
    RA, RB, DA, DB, SA, SB, QA, QR, T, TR,
    lsem, osem, ws, wr, ys, yr, sqs, sqr, ins, inr, gxs, gxr, gzs, gzr,
    xs, xr, qs, qr, ts, tr,
):
    dp, mp = lax.axis_index("dp"), lax.axis_index("mp")
    x, z = lax.div(dp, NZ), rem(dp, NZ)
    y, c = lax.div(mp, 2), rem(mp, 2)
    pending = []

    def to_x(k):
        return (rem(x + k, NX) * NZ + z, mp)

    def to_z(k):
        return (x * NZ + rem(z + k, NZ), mp)

    def to_y(k):
        return (dp, rem(y + k, NY) * 2 + c)

    def to_mp(k):
        return (dp, rem(mp + k, 8))

    sibling = (dp, 2 * y + 1 - c)

    def send(src, dst, ss, rs, dev):
        copy = pltpu.make_async_remote_copy(
            src_ref=src, dst_ref=dst, send_sem=ss, recv_sem=rs, device_id=dev, device_id_type=MESH
        )
        copy.start()
        pending.append(copy)

    def arrived(dst, ss, rs, dev):
        pltpu.make_async_remote_copy(
            src_ref=dst, dst_ref=dst, send_sem=ss, recv_sem=rs, device_id=dev, device_id_type=MESH
        ).wait_recv()

    get_kg = pltpu.make_async_copy(kg_in, KG, lsem.at[0])
    get_x = pltpu.make_async_copy(x_in, X, lsem.at[1])
    get_w = pltpu.make_async_copy(w_in, WR.at[0, 0, 0], lsem.at[2])
    get_gain = pltpu.make_async_copy(gain_in, gain, lsem.at[3])
    get_picked = pltpu.make_async_copy(picked_in, picked, lsem.at[4])
    get_kg.start()
    get_w.start()
    get_x.start()
    get_gain.start()
    get_picked.start()

    barrier = pltpu.get_barrier_semaphore()
    for k in range(1, NZ):
        pl.semaphore_signal(barrier, inc=1, device_id=to_z(k), device_id_type=MESH)
    for k in range(1, NX):
        pl.semaphore_signal(barrier, inc=1, device_id=to_x(k), device_id_type=MESH)
    for k in range(1, 8):
        pl.semaphore_signal(barrier, inc=1, device_id=to_mp(k), device_id_type=MESH)

    get_kg.wait()

    def flip(j, _):
        rows = pl.ds(pl.multiple_of(j * 128, 128), 128)
        GT[mp, :, rows] = KG[rows, :].T
        return 0

    lax.fori_loop(0, 8, flip, 0)
    get_w.wait()
    pl.semaphore_wait(barrier, 7 + NX - 1 + NZ - 1)

    whole, low, high = slice(None), pl.ds(0, 512), pl.ds(512, 512)
    later = pl.ds(1, 3)

    def w_send(i, src, dst, dev, cols=whole):
        send(WR.at[(*src, whole, cols)], WR.at[(*dst, whole, cols)], ws.at[i], wr.at[i], dev)

    def w_arrived(i, dst, cols=whole):
        arrived(WR.at[(*dst, whole, cols)], ws.at[i], wr.at[i], to_x(1))

    near = ((1, 15), (3, 1), (2, 14))

    def w_cross(i, j, m):
        w_send(i, (0, j, m), (1, j, m), to_x(3))
        w_send(i + 1, (0, j, m), (3, j, m), to_x(1))

    def w_relay(i, j, m):
        w_arrived(i, (1, j, m))
        w_send(i + 2, (1, j, m), (2, j, m), to_x(3), low)
        w_arrived(i + 1, (3, j, m))
        w_send(i + 3, (3, j, m), (2, j, m), to_x(1), high)

    def w_relayed(i, j, m):
        w_arrived(i + 2, (2, j, m), low)
        w_arrived(i + 3, (2, j, m), high)

    for i, (j, k) in enumerate(near):
        w_send(i, (0, 0, 0), (0, j, 0), to_z(k))
    w_cross(10, 0, 0)
    for m in (1, 3, 2):
        w_send(2 + m, (0, 0, 0), (0, 0, m), to_z(16 - 4 * m))

    def block(k, other=False):
        return rem(y + k, NY) * 2 + ((1 - c) if other else c)

    def half(b, h):
        return GT.at[b, pl.ds(64 * h, 64), :]

    send(half(mp, 0), half(mp, 0), ys.at[1], yr.at[1], to_y(1))
    send(half(mp, 1), half(mp, 1), ys.at[3], yr.at[3], to_y(3))
    send(half(mp, 1), half(mp, 1), ys.at[2], yr.at[2], to_y(1))
    send(half(mp, 0), half(mp, 0), ys.at[4], yr.at[4], to_y(3))
    send(GT.at[mp], GT.at[mp], ys.at[0], yr.at[0], sibling)

    eye = lax.broadcasted_iota(jnp.int32, (128, 128), 0) == lax.broadcasted_iota(
        jnp.int32, (128, 128), 1
    )

    def to_row(col):
        return jnp.sum(jnp.where(eye, col, 0.0), axis=0, keepdims=True)

    def to_col(row):
        return jnp.sum(jnp.where(eye, row, 0.0), axis=1, keepdims=True)

    get_x.wait()

    def squares(j, _):
        rows = X[pl.ds(pl.multiple_of(j * 128, 128), 128), :].astype(F32)
        SQ[mp, pl.ds(j, 1), :] = to_row(jnp.sum(rows * rows, axis=1, keepdims=True))
        return 0

    lax.fori_loop(0, 8, squares, 0)
    for k in range(1, 8):
        send(SQ.at[mp], SQ.at[mp], sqs.at[k], sqr.at[k], to_mp(k))

    get_picked.wait()
    get_gain.wait()
    live = lax.broadcasted_iota(jnp.int32, (1, 1024), 1) < count[0]
    wanted = jnp.where(live, picked[...], -1)

    def selected(j, _):
        number = lax.broadcasted_iota(jnp.int32, (128, 1024), 0) + j * 128
        hit = jnp.where(wanted == number, 1.0, 0.0)
        inv_c[pl.ds(pl.multiple_of(j * 128, 128), 128), :] = jnp.sum(hit, axis=1, keepdims=True)
        return 0

    lax.fori_loop(0, 8, selected, 0)

    for i, (j, k) in enumerate(near):
        w_arrived(i, (0, j, 0))
    w_cross(14, pl.ds(1, 3), 0)
    w_relay(10, 0, 0)

    for k in range(1, 8):
        arrived(SQ.at[rem(mp + 8 - k, 8)], sqs.at[k], sqr.at[k], to_mp(8 - k))
    total = SQ[0]
    for k in range(1, 8):
        total = total + SQ[k]
    SQ[8] = lax.rsqrt(total / D + EPS)

    def hidden(j, _):
        rows = pl.ds(pl.multiple_of(j * 128, 128), 128)
        inverse = to_col(SQ[8, pl.ds(j, 1), :]) * inv_c[rows, :]
        inv_c[rows, :] = inverse
        normed = X[rows, :].astype(F32) * inverse
        H[rows, :] = (normed * gain[...]).astype(BF16)
        return 0

    arrived(half(block(3), 0), ys.at[1], yr.at[1], to_y(3))
    send(half(block(3), 0), half(block(3), 0), ys.at[5], yr.at[5], to_y(1))
    arrived(half(block(1), 1), ys.at[3], yr.at[3], to_y(1))
    send(half(block(1), 1), half(block(1), 1), ys.at[6], yr.at[6], to_y(3))
    lax.fori_loop(0, 8, hidden, 0)
    arrived(half(block(3), 1), ys.at[2], yr.at[2], to_y(3))
    send(GT.at[block(3)], GT.at[block(3)], ys.at[7], yr.at[7], sibling)
    arrived(half(block(1), 0), ys.at[4], yr.at[4], to_y(1))
    send(GT.at[block(1)], GT.at[block(1)], ys.at[8], yr.at[8], sibling)

    for m in (1, 3, 2):
        w_arrived(2 + m, (0, 0, m))
    for i, (j, k) in enumerate(near):
        w_send(6 + i, (0, 0, later), (0, j, later), to_z(k))
    w_cross(18, 0, later)
    w_relay(14, pl.ds(1, 3), 0)
    arrived(half(block(2), 0), ys.at[5], yr.at[5], to_y(3))
    arrived(half(block(2), 1), ys.at[6], yr.at[6], to_y(1))
    send(GT.at[block(2)], GT.at[block(2)], ys.at[9], yr.at[9], sibling)
    arrived(GT.at[block(0, True)], ys.at[0], yr.at[0], sibling)
    arrived(GT.at[block(3, True)], ys.at[7], yr.at[7], sibling)
    arrived(GT.at[block(1, True)], ys.at[8], yr.at[8], sibling)
    arrived(GT.at[block(2, True)], ys.at[9], yr.at[9], sibling)

    def x_send(i, p, src, dst, d):
        send(src.at[p], dst.at[p], xs.at[i, p, d], xr.at[i, p, d], to_x(1 if d == 0 else 3))

    def x_arrived(i, p, dst, d):
        arrived(dst.at[p], xs.at[i, p, d], xr.at[i, p, d], to_x(3 if d == 0 else 1))

    def terms(p):
        def product(k):
            b = rem(x + k, NX)
            lhs = GT[pl.ds(2 * b, 2)].reshape(256, 1024)
            out = dot(lhs, H[:, 256 * p : 256 * p + 256])
            return out[:, :128].reshape(16, 16, 128), out[:, 128:].reshape(16, 16, 128)

        left, right = product(2)
        S2[p, 0] = left.astype(BF16)
        S2[p, 1] = right.astype(BF16)
        send(S2.at[p, 0], RA.at[p], xs.at[0, p, 0], xr.at[0, p, 0], to_x(1))
        send(S2.at[p, 1], RB.at[p], xs.at[0, p, 1], xr.at[0, p, 1], to_x(3))
        left, right = product(1)
        F1[p] = left
        D1[p] = right.astype(BF16)
        x_send(1, p, D1, DB, 0)
        left, right = product(3)
        D3[p] = left.astype(BF16)
        F3[p] = right
        x_send(1, p, D3, DA, 1)
        left, right = product(0)
        R[p, :, :, :, :128] = left.reshape(4, 4, 16, 128)
        R[p, :, :, :, 128:] = right.reshape(4, 4, 16, 128)

    def relay(p):
        x_arrived(0, p, RA, 0)
        U1[p] = (F1[p] + RA[p].astype(F32)).astype(BF16)
        x_send(2, p, U1, SA, 0)
        x_arrived(0, p, RB, 1)
        U3[p] = (F3[p] + RB[p].astype(F32)).astype(BF16)
        x_send(2, p, U3, SB, 1)

    ways = ((1, 15), (15, 1), (2, 14))

    def owned(p):
        x_arrived(1, p, DB, 0)
        x_arrived(1, p, DA, 1)
        x_arrived(2, p, SA, 0)
        x_arrived(2, p, SB, 1)
        for cols, first, second in ((slice(0, 128), DA, SA), (slice(128, 256), DB, SB)):
            more = first[p].astype(F32) + second[p].astype(F32)
            R[p, :, :, :, cols] = R[p, :, :, :, cols] + more.reshape(4, 4, 16, 128)
        for i, (k, _) in enumerate(ways):
            QA[p, i] = R[p, :, rem(z + k, 4)].astype(BF16)
            send(QA.at[p, i], QR.at[p, i], qs.at[p, i], qr.at[p, i], to_z(k))

    def fourth(p):
        sums = R[p, :, rem(z, 4)]
        for i, (_, k) in enumerate(ways):
            arrived(QR.at[p, i], qs.at[p, i], qr.at[p, i], to_z(k))
            sums = sums + QR[p, i].astype(F32)
        T[p] = sums
        for m in (1, 3, 2):
            mine = T.at[p, rem(lax.div(z, 4) + m, 4)]
            send(mine, TR.at[p, m - 1], ts.at[p, m - 1], tr.at[p, m - 1], to_z(4 * m))

    def complete(p):
        sums = T[p, lax.div(z, 4)]
        for m in (1, 2, 3):
            arrived(TR.at[p, m - 1], ts.at[p, m - 1], tr.at[p, m - 1], to_z(16 - 4 * m))
            sums = sums + TR[p, m - 1]
        wg_out[:, 256 * p : 256 * p + 256] = sums

    def unflip(r, _):
        rows = pl.ds(pl.multiple_of(r * 256, 256), 256)
        G[rows, :] = GT[:, :, rows].reshape(1024, 256).T
        return 0

    def backward(r):
        rows = pl.ds(256 * r, 256)

        def tile(n, _):
            here = pl.ds(pl.multiple_of(n * 256, 256), 256)
            GH[rows, here] = dot(G[rows, :], W[:, :, here].reshape(1024, 256))
            return 0

        lax.fori_loop(0, 4, tile, 0)
        for i in (0, 1):
            j = 2 * r + i
            part = pl.ds(128 * j, 128)
            normed = X[part, :].astype(F32) * inv_c[part, :]
            product = GH[part, :] * normed
            sums = jnp.sum(product, axis=0, keepdims=True)
            for b in range(8):
                piece = sums[:, 128 * b : 128 * b + 128]
                if j == 0:
                    GX[x, b : b + 1, :] = piece
                else:
                    GX[x, b : b + 1, :] = GX[x, b : b + 1, :] + piece
            inner = jnp.sum(gain[...] * product, axis=1, keepdims=True)
            IN[mp, j : j + 1, :] = to_row(inner)

    def w_place(i, j, m):
        there = rem(x + i, NX) * NZ + rem(z + NZ + (0, 1, 2, -1)[j] + 4 * m, NZ)
        W[there] = WR[i, j, m]

    terms(0)
    terms(1)
    for i, (j, k) in enumerate(near):
        w_arrived(6 + i, (0, j, later))
        w_cross(22 + 4 * i, j, later)
    w_relay(18, 0, later)
    terms(2)
    relay(0)
    terms(3)
    relay(1)
    lax.fori_loop(0, 4, unflip, 0)
    owned(0)
    relay(2)
    for i, (j, k) in enumerate(near):
        w_relay(22 + 4 * i, j, later)
    owned(1)
    fourth(0)
    relay(3)
    for j in range(4):
        for m in range(4):
            w_place(0, j, m)
            if j == 0 or m == 0:
                w_place(1, j, m)
                w_place(3, j, m)
    w_relayed(10, 0, 0)
    w_relayed(14, pl.ds(1, 3), 0)
    w_relayed(18, 0, later)
    for i, (j, k) in enumerate(near):
        w_relayed(22 + 4 * i, j, later)
    for j in range(4):
        for m in range(4):
            w_place(2, j, m)
            if j != 0 and m != 0:
                w_place(1, j, m)
                w_place(3, j, m)
    backward(0)
    owned(2)
    fourth(1)
    backward(1)
    owned(3)
    fourth(2)
    backward(2)
    fourth(3)
    backward(3)
    for k in range(1, 8):
        send(IN.at[mp], IN.at[mp], ins.at[k], inr.at[k], to_mp(k))
    for k in range(1, NX):
        send(GX.at[x], GX.at[x], gxs.at[k], gxr.at[k], to_x(k))
    complete(0)
    complete(1)

    def column(r, i):
        return to_col(picked[:, 256 * r + 128 * i : 256 * r + 128 * i + 128].astype(F32))

    def choose(r):
        ids = jnp.concatenate([column(r, 0), column(r, 1)], axis=0).astype(jnp.int32)
        slot = lax.broadcasted_iota(jnp.int32, (256, 1), 0) + 256 * r
        ids = jnp.where(slot < count[0], ids, -1)
        number = lax.broadcasted_iota(jnp.int32, (256, 1024), 1)
        H[pl.ds(256 * r, 256), :] = jnp.where(ids == number, 1.0, 0.0).astype(BF16)

    for r in range(4):
        choose(r)
    for k in range(1, NX):
        arrived(GX.at[rem(x + NX - k, NX)], gxs.at[k], gxr.at[k], to_x(NX - k))
    GZ[z] = GX[0] + GX[1] + GX[2] + GX[3]
    for k in range(1, NZ):
        send(GZ.at[z], GZ.at[z], gzs.at[k], gzr.at[k], to_z(k))
    for k in range(1, 8):
        arrived(IN.at[rem(mp + 8 - k, 8)], ins.at[k], inr.at[k], to_mp(8 - k))
    total = IN[0]
    for k in range(1, 8):
        total = total + IN[k]
    IN[8] = total / D

    def finish(j, _):
        rows = pl.ds(pl.multiple_of(j * 128, 128), 128)
        inner = to_col(IN[8, pl.ds(j, 1), :])
        inverse = inv_c[rows, :]
        normed = X[rows, :].astype(F32) * inverse
        RG[rows, :] = (inverse * (gain[...] * GH[rows, :] - normed * inner)).astype(BF16)
        return 0

    lax.fori_loop(0, 8, finish, 0)

    def place(r):
        rows = pl.ds(256 * r, 256)

        def tile(n, _):
            here = pl.ds(pl.multiple_of(n * 256, 256), 256)
            OUT[rows, here] = dot(H[rows, :], RG[:, here]).astype(BF16)
            return 0

        lax.fori_loop(0, 4, tile, 0)
        copy = pltpu.make_async_copy(OUT.at[rows], rows_out.at[rows], osem.at[r])
        copy.start()
        return copy

    written = [place(r) for r in range(4)]
    complete(2)
    complete(3)
    for k in range(1, NZ):
        arrived(GZ.at[rem(z + NZ - k, NZ)], gzs.at[k], gzr.at[k], to_z(NZ - k))
    total = GZ[0]
    for k in range(1, NZ):
        total = total + GZ[k]
    gg_out[...] = total
    for copy in written:
        copy.wait()
    for copy in pending:
        copy.wait_send()


def deliver(rows_in, wg_in, gg_in, rows_out, wg_out, gg_out, sem):
    copies = [
        pltpu.make_async_copy(wg_in, wg_out, sem.at[8]),
        pltpu.make_async_copy(gg_in, gg_out, sem.at[9]),
    ]
    for i in range(8):
        part = pl.ds(128 * i, 128)
        copies.append(pltpu.make_async_copy(rows_in.at[part], rows_out.at[part], sem.at[i]))
    for copy in copies:
        copy.start()
    for copy in copies:
        copy.wait()


def shards(checkpoint, key_grads, key_weight, norm_gain, picked_rows, row_counts):
    any_space = pl.BlockSpec(memory_space=pl.ANY)
    vmem = pl.BlockSpec(memory_space=pltpu.VMEM)
    smem = pl.BlockSpec(memory_space=pltpu.SMEM)
    dma = pltpu.SemaphoreType.DMA
    piece = (4, 16, 16, 128)
    scratch = [
        pltpu.VMEM((1024, 1024), BF16),
        pltpu.VMEM((1024, 128), BF16),
        pltpu.VMEM((8, 128, 1024), BF16),
        pltpu.VMEM((1024, 1024), BF16),
        pltpu.VMEM((NX, 4, 4, 16, 1024), BF16),
        pltpu.VMEM((NX * NZ, 16, 1024), BF16),
        pltpu.VMEM((1024, 1024), BF16),
        pltpu.VMEM((1024, 1024), F32),
        pltpu.VMEM((1024, 1024), BF16),
        pltpu.VMEM((1024, 1024), BF16),
        pltpu.VMEM((1, 1024), F32),
        pltpu.VMEM((1, 1024), jnp.int32),
        pltpu.VMEM((1024, 1), F32),
        pltpu.VMEM((9, 8, 128), F32),
        pltpu.VMEM((9, 8, 128), F32),
        pltpu.VMEM((NX, 8, 128), F32),
        pltpu.VMEM((NZ, 8, 128), F32),
        pltpu.VMEM((4, 2, 16, 16, 128), BF16),
        pltpu.VMEM(piece, BF16),
        pltpu.VMEM(piece, BF16),
        pltpu.VMEM(piece, F32),
        pltpu.VMEM(piece, F32),
        pltpu.VMEM(piece, BF16),
        pltpu.VMEM(piece, BF16),
        pltpu.VMEM((4, 4, 4, 16, 256), F32),
        *[pltpu.VMEM(piece, BF16) for _ in range(6)],
        pltpu.VMEM((4, 3, 4, 16, 256), BF16),
        pltpu.VMEM((4, 3, 4, 16, 256), BF16),
        pltpu.VMEM((4, 4, 16, 256), F32),
        pltpu.VMEM((4, 3, 16, 256), F32),
        dma((5,)), dma((4,)),
        dma((34,)), dma((34,)),
        dma((10,)), dma((10,)),
        dma((8,)), dma((8,)),
        dma((8,)), dma((8,)),
        dma((NX,)), dma((NX,)),
        dma((NZ,)), dma((NZ,)),
        dma((3, 4, 2)), dma((3, 4, 2)),
        dma((4, 3)), dma((4, 3)),
        dma((4, 3)), dma((4, 3)),
    ]
    row_grads, weight_grad, gain_grad = pl.pallas_call(
        kernel,
        out_shape=(
            jax.ShapeDtypeStruct((1024, 1024), BF16),
            jax.ShapeDtypeStruct((16, 1024), F32),
            jax.ShapeDtypeStruct((8, 128), F32),
        ),
        in_specs=[any_space] * 5 + [smem],
        out_specs=(any_space, vmem, vmem),
        scratch_shapes=scratch,
        compiler_params=pltpu.CompilerParams(
            collective_id=0, has_side_effects=True, vmem_limit_bytes=60 * 1024 * 1024
        ),
        cost_estimate=pl.CostEstimate(flops=6 * 1024**3, bytes_accessed=8 * 1024**2, transcendentals=1024),
        name="norm_key_backward",
    )(checkpoint, key_grads, key_weight, norm_gain.reshape(1, 1024), picked_rows, row_counts)
    row_grads, weight_grad, gain_grad = pl.pallas_call(
        deliver,
        out_shape=(
            jax.ShapeDtypeStruct((1024, 1024), BF16),
            jax.ShapeDtypeStruct((16, 1024), F32),
            jax.ShapeDtypeStruct((8, 128), F32),
        ),
        in_specs=[any_space] * 3,
        out_specs=(any_space,) * 3,
        scratch_shapes=[dma((10,))],
        name="deliver",
    )(row_grads, weight_grad, gain_grad)
    return row_grads, weight_grad, gain_grad.reshape(1024)


def solution(mesh):
    in_specs = (P("dp", "mp"), P("dp", "mp"), P("dp", "mp"), P("mp"), P("dp", None), P("dp"))
    out_specs = (P("dp", "mp"), P("dp", "mp"), P("mp"))
    return jax.shard_map(shards, mesh=mesh, in_specs=in_specs, out_specs=out_specs, check_vma=False)
```

time: 98.5 us -> 160 us (1.62)
  Pallas kernels: 89.6 us -> 158 us
  local copies, waits for them, and re-layouts: 7.21 us -> 0 us
    pallas_call x0 -> x1, Pallas kernels: none -> 66.8 us  [shards(): pl.pallas_call(deliver, out_shape=(jax.ShapeDtypeStruct((1024, 1024), BF1...]
    unnamed x13 -> x0, local copies, waits for them, and re-layouts: 7.21 us -> none
    pallas_call x1, Pallas kernels: 89.6 us -> 91.3 us  [shards(): pl.pallas_call(kernel, out_shape=(jax.ShapeDtypeStruct((1024, 1024), BF16...]
where the time goes in v2:
time: 160 us; the launch traced here: 159 us
  Pallas kernels  158 us (99%)
    pallas_call x1, Pallas kernels, shards(): pl.pallas_call(kernel, out_shape=(jax.ShapeDtypeStruct((1024, 1024), BF16...  91.3 us
    pallas_call x1, Pallas kernels, shards(): pl.pallas_call(deliver, out_shape=(jax.ShapeDtypeStruct((1024, 1024), BF1...  66.8 us

profile of v2, /device:TPU:1, one launch (start us, length us, event | category | flops | bytes accessed | tf_op | source)
XLA Modules:
  0.0 159.4 jit_solution(4000102912802431988)
XLA Ops:
  1.3 91.3 %norm_key_backward.1 = (bf16[1024,1024]{1,0:T(8,128)(2,1)}, f32[16,1024]{1,0:T(8,128)}, f32[8,128]{1,0:T(8,128)}) custom-call(bf16[1024,1024]{1,0:T(8,128)(2,1)} %x_in.1, bf16[1024,128]{1,0:T(8,128)(2,1)} %kg_in.1, bf16[16,1024]{1,0:T(8,128)(2,1)} %w_in.1, f32[1,1024]{1,0:T(1,128)} %bitcast.2, s32[1,1024]{1,0:T(1,128)} %picked_in.1, s32[1]{0:T(128)S(6)} %copy.9.count), custom_call_target="tpu_custom_call" | custom-call | flops 6442450944 | bytes 8388608 | tf_op jit(solution)/shard_map/norm_key_backward/pallas_call | solution.py:495
  92.5 66.8 %deliver.1 = (bf16[1024,1024]{1,0:T(8,128)(2,1)}, f32[16,1024]{1,0:T(8,128)}, f32[8,128]{1,0:T(8,128)}) custom-call(bf16[1024,1024]{1,0:T(8,128)(2,1)} %get-tuple-element.9.rows_in, f32[16,1024]{1,0:T(8,128)} %get-tuple-element.10.wg_in, f32[8,128]{1,0:T(8,128)} %get-tuple-element.11.gg_in), custom_call_target="tpu_custom_call" | custom-call | tf_op jit(solution)/shard_map/deliver/pallas_call | solution.py:511

commit v3 on v2

--- a/solution.py
+++ b/solution.py
@@ -23,12 +23,12 @@
 
 
 def kernel(
-    x_in, kg_in, w_in, gain_in, picked_in, count,
+    x_in, kg_in, w_in, gain_in, picked_in, count_in,
     rows_out, wg_out, gg_out,
     X, KG, GT, G, WR, W, H, GH, RG, OUT,
-    gain, picked, inv_c,
+    gain, picked, count, inv_c,
     SQ, IN, GX, GZ,
-    S2, D1, D3, F1, F3, U1, U3, R,
+    S2, D1, D3, F1, F3, V, U1, U3, R,
     RA, RB, DA, DB, SA, SB, QA, QR, T, TR,
     lsem, osem, ws, wr, ys, yr, sqs, sqr, ins, inr, gxs, gxr, gzs, gzr,
     xs, xr, qs, qr, ts, tr,
@@ -69,11 +69,13 @@
     get_w = pltpu.make_async_copy(w_in, WR.at[0, 0, 0], lsem.at[2])
     get_gain = pltpu.make_async_copy(gain_in, gain, lsem.at[3])
     get_picked = pltpu.make_async_copy(picked_in, picked, lsem.at[4])
+    get_count = pltpu.make_async_copy(count_in, count, lsem.at[5])
     get_kg.start()
     get_w.start()
     get_x.start()
     get_gain.start()
     get_picked.start()
+    get_count.start()
 
     barrier = pltpu.get_barrier_semaphore()
     for k in range(1, NZ):
@@ -94,28 +96,34 @@
     get_w.wait()
     pl.semaphore_wait(barrier, 7 + NX - 1 + NZ - 1)
 
-    whole, low, high = slice(None), pl.ds(0, 512), pl.ds(512, 512)
+    whole, most, rest = pl.ds(0, 1024), pl.ds(0, 512), pl.ds(512, 512)
     later = pl.ds(1, 3)
 
     def w_send(i, src, dst, dev, cols=whole):
-        send(WR.at[(*src, whole, cols)], WR.at[(*dst, whole, cols)], ws.at[i], wr.at[i], dev)
+        send(WR.at[(*src, slice(None), cols)], WR.at[(*dst, slice(None), cols)], ws.at[i], wr.at[i], dev)
 
     def w_arrived(i, dst, cols=whole):
-        arrived(WR.at[(*dst, whole, cols)], ws.at[i], wr.at[i], to_x(1))
+        arrived(WR.at[(*dst, slice(None), cols)], ws.at[i], wr.at[i], to_x(1))
 
     near = ((1, 15), (3, 1), (2, 14))
 
-    def w_cross(i, j, m):
-        w_send(i, (0, j, m), (1, j, m), to_x(3))
-        w_send(i + 1, (0, j, m), (3, j, m), to_x(1))
-
-    def w_relay(i, j, m):
-        w_arrived(i, (1, j, m))
+    def w_cross(i, j, m, cols=whole):
+        w_send(i, (0, j, m), (1, j, m), to_x(3), cols)
+        w_send(i + 1, (0, j, m), (3, j, m), to_x(1), cols)
+
+    def halves(cols):
+        size = cols.size // 2
+        return pl.ds(0, size), pl.ds(size, size)
+
+    def w_relay(i, j, m, cols=whole):
+        low, high = halves(cols)
+        w_arrived(i, (1, j, m), cols)
         w_send(i + 2, (1, j, m), (2, j, m), to_x(3), low)
-        w_arrived(i + 1, (3, j, m))
+        w_arrived(i + 1, (3, j, m), cols)
         w_send(i + 3, (3, j, m), (2, j, m), to_x(1), high)
 
-    def w_relayed(i, j, m):
+    def w_relayed(i, j, m, cols=whole):
+        low, high = halves(cols)
         w_arrived(i + 2, (2, j, m), low)
         w_arrived(i + 3, (2, j, m), high)
 
@@ -159,6 +167,7 @@
         send(SQ.at[mp], SQ.at[mp], sqs.at[k], sqr.at[k], to_mp(k))
 
     get_picked.wait()
+    get_count.wait()
     get_gain.wait()
     live = lax.broadcasted_iota(jnp.int32, (1, 1024), 1) < count[0]
     wanted = jnp.where(live, picked[...], -1)
@@ -176,6 +185,10 @@
     w_cross(14, pl.ds(1, 3), 0)
     w_relay(10, 0, 0)
 
+    arrived(half(block(3), 0), ys.at[1], yr.at[1], to_y(3))
+    send(half(block(3), 0), half(block(3), 0), ys.at[5], yr.at[5], to_y(1))
+    arrived(half(block(1), 1), ys.at[3], yr.at[3], to_y(1))
+    send(half(block(1), 1), half(block(1), 1), ys.at[6], yr.at[6], to_y(3))
     for k in range(1, 8):
         arrived(SQ.at[rem(mp + 8 - k, 8)], sqs.at[k], sqr.at[k], to_mp(8 - k))
     total = SQ[0]
@@ -191,10 +204,6 @@
         H[rows, :] = (normed * gain[...]).astype(BF16)
         return 0
 
-    arrived(half(block(3), 0), ys.at[1], yr.at[1], to_y(3))
-    send(half(block(3), 0), half(block(3), 0), ys.at[5], yr.at[5], to_y(1))
-    arrived(half(block(1), 1), ys.at[3], yr.at[3], to_y(1))
-    send(half(block(1), 1), half(block(1), 1), ys.at[6], yr.at[6], to_y(3))
     lax.fori_loop(0, 8, hidden, 0)
     arrived(half(block(3), 1), ys.at[2], yr.at[2], to_y(3))
     send(GT.at[block(3)], GT.at[block(3)], ys.at[7], yr.at[7], sibling)
@@ -236,12 +245,12 @@
         left, right = product(1)
         F1[p] = left
         D1[p] = right.astype(BF16)
-        x_send(1, p, D1, DB, 0)
         left, right = product(3)
         D3[p] = left.astype(BF16)
         F3[p] = right
-        x_send(1, p, D3, DA, 1)
         left, right = product(0)
+        V[p, 0] = left
+        V[p, 1] = right
         R[p, :, :, :, :128] = left.reshape(4, 4, 16, 128)
         R[p, :, :, :, 128:] = right.reshape(4, 4, 16, 128)
 
@@ -249,9 +258,11 @@
         x_arrived(0, p, RA, 0)
         U1[p] = (F1[p] + RA[p].astype(F32)).astype(BF16)
         x_send(2, p, U1, SA, 0)
+        x_send(1, p, D1, DB, 0)
         x_arrived(0, p, RB, 1)
         U3[p] = (F3[p] + RB[p].astype(F32)).astype(BF16)
         x_send(2, p, U3, SB, 1)
+        x_send(1, p, D3, DA, 1)
 
     ways = ((1, 15), (15, 1), (2, 14))
 
@@ -289,84 +300,30 @@
         G[rows, :] = GT[:, :, rows].reshape(1024, 256).T
         return 0
 
-    def backward(r):
-        rows = pl.ds(256 * r, 256)
-
-        def tile(n, _):
-            here = pl.ds(pl.multiple_of(n * 256, 256), 256)
-            GH[rows, here] = dot(G[rows, :], W[:, :, here].reshape(1024, 256))
-            return 0
-
-        lax.fori_loop(0, 4, tile, 0)
-        for i in (0, 1):
-            j = 2 * r + i
-            part = pl.ds(128 * j, 128)
-            normed = X[part, :].astype(F32) * inv_c[part, :]
-            product = GH[part, :] * normed
-            sums = jnp.sum(product, axis=0, keepdims=True)
-            for b in range(8):
-                piece = sums[:, 128 * b : 128 * b + 128]
-                if j == 0:
-                    GX[x, b : b + 1, :] = piece
-                else:
-                    GX[x, b : b + 1, :] = GX[x, b : b + 1, :] + piece
-            inner = jnp.sum(gain[...] * product, axis=1, keepdims=True)
-            IN[mp, j : j + 1, :] = to_row(inner)
+    def backward(n):
+        here = pl.ds(256 * n, 256)
+        GH[:, here] = dot(G[...], W[:, :, here].reshape(1024, 256))
+
+    def entered(j):
+        part = pl.ds(128 * j, 128)
+        normed = X[part, :].astype(F32) * inv_c[part, :]
+        inner = jnp.sum(gain[...] * GH[part, :] * normed, axis=1, keepdims=True)
+        IN[mp, j : j + 1, :] = to_row(inner)
+
+    def gain_terms(p):
+        for h, kept in enumerate(((V.at[p, 0], F1, S2.at[p, 0], D3), (V.at[p, 1], D1, S2.at[p, 1], F3))):
+            b = 2 * p + h
+            cols = pl.ds(128 * b, 128)
+            sums = jnp.zeros((1, 128), F32)
+            for k, ref in enumerate(kept):
+                term = (ref[p] if k % 2 else ref[...]).astype(F32)
+                rows = W[pl.ds(16 * rem(x + k, NX), 16), :, cols].astype(F32)
+                sums = sums + jnp.sum((rows * term).reshape(256, 128), axis=0, keepdims=True)
+            GX[x, b : b + 1, :] = sums / gain[:, cols]
 
     def w_place(i, j, m):
         there = rem(x + i, NX) * NZ + rem(z + NZ + (0, 1, 2, -1)[j] + 4 * m, NZ)
         W[there] = WR[i, j, m]
-
-    terms(0)
-    terms(1)
-    for i, (j, k) in enumerate(near):
-        w_arrived(6 + i, (0, j, later))
-        w_cross(22 + 4 * i, j, later)
-    w_relay(18, 0, later)
-    terms(2)
-    relay(0)
-    terms(3)
-    relay(1)
-    lax.fori_loop(0, 4, unflip, 0)
-    owned(0)
-    relay(2)
-    for i, (j, k) in enumerate(near):
-        w_relay(22 + 4 * i, j, later)
-    owned(1)
-    fourth(0)
-    relay(3)
-    for j in range(4):
-        for m in range(4):
-            w_place(0, j, m)
-            if j == 0 or m == 0:
-                w_place(1, j, m)
-                w_place(3, j, m)
-    w_relayed(10, 0, 0)
-    w_relayed(14, pl.ds(1, 3), 0)
-    w_relayed(18, 0, later)
-    for i, (j, k) in enumerate(near):
-        w_relayed(22 + 4 * i, j, later)
-    for j in range(4):
-        for m in range(4):
-            w_place(2, j, m)
-            if j != 0 and m != 0:
-                w_place(1, j, m)
-                w_place(3, j, m)
-    backward(0)
-    owned(2)
-    fourth(1)
-    backward(1)
-    owned(3)
-    fourth(2)
-    backward(2)
-    fourth(3)
-    backward(3)
-    for k in range(1, 8):
-        send(IN.at[mp], IN.at[mp], ins.at[k], inr.at[k], to_mp(k))
-    for k in range(1, NX):
-        send(GX.at[x], GX.at[x], gxs.at[k], gxr.at[k], to_x(k))
-    complete(0)
-    complete(1)
 
     def column(r, i):
         return to_col(picked[:, 256 * r + 128 * i : 256 * r + 128 * i + 128].astype(F32))
@@ -378,13 +335,76 @@
         number = lax.broadcasted_iota(jnp.int32, (256, 1024), 1)
         H[pl.ds(256 * r, 256), :] = jnp.where(ids == number, 1.0, 0.0).astype(BF16)
 
+    across = pl.ds(1, 3)
+
+    def last_cross(i):
+        w_arrived(6 + i, (0, near[i][0], later))
+        w_cross(22 + 4 * i, near[i][0], later, most)
+
+    terms(0)
+    w_relayed(10, 0, 0)
+    terms(1)
+    w_relay(18, 0, later)
+    w_relayed(14, pl.ds(1, 3), 0)
+    terms(2)
+    relay(0)
+    terms(3)
+    w_relayed(18, 0, later)
+    for i, (j, k) in enumerate(near):
+        w_send(34 + i, (across, 0, later), (across, j, later), to_z(k), rest)
+    relay(1)
+    last_cross(0)
+    relay(2)
+    last_cross(1)
+    lax.fori_loop(0, 4, unflip, 0)
+    owned(0)
+    relay(3)
+    last_cross(2)
+    for j in range(4):
+        for m in range(4):
+            w_place(0, j, m)
+            if j == 0 or m == 0:
+                for i in (1, 2, 3):
+                    w_place(i, j, m)
+    owned(1)
+    fourth(0)
+    w_relay(22, near[0][0], later, most)
     for r in range(4):
         choose(r)
+    owned(2)
+    fourth(1)
+    w_relay(26, near[1][0], later, most)
+    w_relay(30, near[2][0], later, most)
+    for i, (j, k) in enumerate(near):
+        w_arrived(34 + i, (across, j, later), rest)
+    owned(3)
+    for i, (j, k) in enumerate(near):
+        w_relayed(22 + 4 * i, j, later, most)
+    for j in (1, 2, 3):
+        for m in (1, 2, 3):
+            for i in (1, 2, 3):
+                w_place(i, j, m)
+    for p in range(4):
+        gain_terms(p)
+    for k in range(1, NX):
+        send(GX.at[x], GX.at[x], gxs.at[k], gxr.at[k], to_x(k))
+    fourth(2)
+    backward(0)
+    backward(1)
+    fourth(3)
+    backward(2)
+    backward(3)
+    for j in range(8):
+        entered(j)
+    for k in range(1, 8):
+        send(IN.at[mp], IN.at[mp], ins.at[k], inr.at[k], to_mp(k))
     for k in range(1, NX):
         arrived(GX.at[rem(x + NX - k, NX)], gxs.at[k], gxr.at[k], to_x(NX - k))
     GZ[z] = GX[0] + GX[1] + GX[2] + GX[3]
     for k in range(1, NZ):
         send(GZ.at[z], GZ.at[z], gzs.at[k], gzr.at[k], to_z(k))
+    complete(0)
+    complete(1)
     for k in range(1, 8):
         arrived(IN.at[rem(mp + 8 - k, 8)], ins.at[k], inr.at[k], to_mp(8 - k))
     total = IN[0]
@@ -402,16 +422,10 @@
 
     lax.fori_loop(0, 8, finish, 0)
 
-    def place(r):
-        rows = pl.ds(256 * r, 256)
-
-        def tile(n, _):
-            here = pl.ds(pl.multiple_of(n * 256, 256), 256)
-            OUT[rows, here] = dot(H[rows, :], RG[:, here]).astype(BF16)
-            return 0
-
-        lax.fori_loop(0, 4, tile, 0)
-        copy = pltpu.make_async_copy(OUT.at[rows], rows_out.at[rows], osem.at[r])
+    def place(n):
+        here = pl.ds(256 * n, 256)
+        OUT[:, here] = dot(H[...], RG[:, here]).astype(BF16)
+        copy = pltpu.make_async_copy(OUT.at[:, here], rows_out.at[:, here], osem.at[n])
         copy.start()
         return copy
 
@@ -430,24 +444,29 @@
         copy.wait_send()
 
 
-def deliver(rows_in, wg_in, gg_in, rows_out, wg_out, gg_out, sem):
-    copies = [
-        pltpu.make_async_copy(wg_in, wg_out, sem.at[8]),
-        pltpu.make_async_copy(gg_in, gg_out, sem.at[9]),
+def deliver(rows_in, wg_in, gg_in, rows_out, wg_out, gg_out, rows, wg, gg, sem):
+    def move(i, src, by, dst):
+        return (
+            pltpu.make_async_copy(src, by, sem.at[0, i]),
+            pltpu.make_async_copy(by, dst, sem.at[1, i]),
+        )
+
+    moves = [
+        move(i, *(ref.at[pl.ds(128 * i, 128)] for ref in (rows_in, rows, rows_out))) for i in range(8)
     ]
-    for i in range(8):
-        part = pl.ds(128 * i, 128)
-        copies.append(pltpu.make_async_copy(rows_in.at[part], rows_out.at[part], sem.at[i]))
-    for copy in copies:
-        copy.start()
-    for copy in copies:
-        copy.wait()
+    moves += [move(8, wg_in, wg, wg_out), move(9, gg_in, gg, gg_out)]
+    for first, _ in moves:
+        first.start()
+    for first, second in moves:
+        first.wait()
+        second.start()
+    for _, second in moves:
+        second.wait()
 
 
 def shards(checkpoint, key_grads, key_weight, norm_gain, picked_rows, row_counts):
     any_space = pl.BlockSpec(memory_space=pl.ANY)
     vmem = pl.BlockSpec(memory_space=pltpu.VMEM)
-    smem = pl.BlockSpec(memory_space=pltpu.SMEM)
     dma = pltpu.SemaphoreType.DMA
     piece = (4, 16, 16, 128)
     scratch = [
@@ -463,6 +482,7 @@
         pltpu.VMEM((1024, 1024), BF16),
         pltpu.VMEM((1, 1024), F32),
         pltpu.VMEM((1, 1024), jnp.int32),
+        pltpu.SMEM((1,), jnp.int32),
         pltpu.VMEM((1024, 1), F32),
         pltpu.VMEM((9, 8, 128), F32),
         pltpu.VMEM((9, 8, 128), F32),
@@ -473,6 +493,7 @@
         pltpu.VMEM(piece, BF16),
         pltpu.VMEM(piece, F32),
         pltpu.VMEM(piece, F32),
+        pltpu.VMEM((4, 2, 16, 16, 128), F32),
         pltpu.VMEM(piece, BF16),
         pltpu.VMEM(piece, BF16),
         pltpu.VMEM((4, 4, 4, 16, 256), F32),
@@ -481,8 +502,8 @@
         pltpu.VMEM((4, 3, 4, 16, 256), BF16),
         pltpu.VMEM((4, 4, 16, 256), F32),
         pltpu.VMEM((4, 3, 16, 256), F32),
-        dma((5,)), dma((4,)),
-        dma((34,)), dma((34,)),
+        dma((6,)), dma((4,)),
+        dma((37,)), dma((37,)),
         dma((10,)), dma((10,)),
         dma((8,)), dma((8,)),
         dma((8,)), dma((8,)),
@@ -499,7 +520,7 @@
             jax.ShapeDtypeStruct((16, 1024), F32),
             jax.ShapeDtypeStruct((8, 128), F32),
         ),
-        in_specs=[any_space] * 5 + [smem],
+        in_specs=[any_space] * 6,
         out_specs=(any_space, vmem, vmem),
         scratch_shapes=scratch,
         compiler_params=pltpu.CompilerParams(
@@ -517,7 +538,13 @@
         ),
         in_specs=[any_space] * 3,
         out_specs=(any_space,) * 3,
-        scratch_shapes=[dma((10,))],
+        scratch_shapes=[
+            pltpu.VMEM((1024, 1024), BF16),
+            pltpu.VMEM((16, 1024), F32),
+            pltpu.VMEM((8, 128), F32),
+            dma((2, 10)),
+        ],
+        compiler_params=pltpu.CompilerParams(vmem_limit_bytes=60 * 1024 * 1024),
         name="deliver",
     )(row_grads, weight_grad, gain_grad)
     return row_grads, weight_grad, gain_grad.reshape(1024)

time: 160 us -> 81.9 us (0.51)
  Pallas kernels: 158 us -> 79.9 us
    pallas_call x1, Pallas kernels: 66.8 us -> 2.45 us  [shards(): pl.pallas_call(deliver, out_shape=(jax.ShapeDtypeStruct((1024, 1024), BF1...]
    pallas_call x1, Pallas kernels: 91.3 us -> 77.5 us  [shards(): pl.pallas_call(kernel, out_shape=(jax.ShapeDtypeStruct((1024, 1024), BF16...]
where the time goes in v3:
time: 81.9 us; the launch traced here: 81.2 us
  Pallas kernels  79.9 us (98%)
  between operations  1.29 us (2%)
    pallas_call x1, Pallas kernels, shards(): pl.pallas_call(kernel, out_shape=(jax.ShapeDtypeStruct((1024, 1024), BF16...  77.5 us
    pallas_call x1, Pallas kernels, shards(): pl.pallas_call(deliver, out_shape=(jax.ShapeDtypeStruct((1024, 1024), BF1...  2.45 us

profile of v3, /device:TPU:1, one launch (start us, length us, event | category | flops | bytes accessed | tf_op | source)
XLA Modules:
  0.0 81.2 jit_solution(14704972730355004944)
XLA Ops:
  1.3 77.5 %norm_key_backward.1 = (bf16[1024,1024]{1,0:T(8,128)(2,1)}, f32[16,1024]{1,0:T(8,128)}, f32[8,128]{1,0:T(8,128)}) custom-call(bf16[1024,1024]{1,0:T(8,128)(2,1)} %x_in.1, bf16[1024,128]{1,0:T(8,128)(2,1)} %kg_in.1, bf16[16,1024]{1,0:T(8,128)(2,1)} %w_in.1, f32[1,1024]{1,0:T(1,128)} %bitcast.2, s32[1,1024]{1,0:T(1,128)} %picked_in.1, s32[1]{0:T(128)S(6)} %copy.9.count_in), custom_call_target="tpu_custom_call" | custom-call | flops 6442450944 | bytes 8388608 | tf_op jit(solution)/shard_map/norm_key_backward/pallas_call | solution.py:516
  78.8 2.4 %deliver.1 = (bf16[1024,1024]{1,0:T(8,128)(2,1)}, f32[16,1024]{1,0:T(8,128)}, f32[8,128]{1,0:T(8,128)}) custom-call(bf16[1024,1024]{1,0:T(8,128)(2,1)} %get-tuple-element.9.rows_in, f32[16,1024]{1,0:T(8,128)} %get-tuple-element.10.wg_in, f32[8,128]{1,0:T(8,128)} %get-tuple-element.11.gg_in), custom_call_target="tpu_custom_call" | custom-call | tf_op jit(solution)/shard_map/deliver/pallas_call | solution.py:532

commit v4 on v3

--- a/solution.py
+++ b/solution.py
@@ -30,8 +30,9 @@
     SQ, IN, GX, GZ,
     S2, D1, D3, F1, F3, V, U1, U3, R,
     RA, RB, DA, DB, SA, SB, QA, QR, T, TR,
+    AZ, QB, QC, Y, ZS, ZR,
     lsem, osem, ws, wr, ys, yr, sqs, sqr, ins, inr, gxs, gxr, gzs, gzr,
-    xs, xr, qs, qr, ts, tr,
+    xs, xr, qs, qr, ts, tr, qbs, qbr, zxs, zxr,
 ):
     dp, mp = lax.axis_index("dp"), lax.axis_index("mp")
     x, z = lax.div(dp, NZ), rem(dp, NZ)
@@ -63,6 +64,10 @@
         pltpu.make_async_remote_copy(
             src_ref=dst, dst_ref=dst, send_sem=ss, recv_sem=rs, device_id=dev, device_id_type=MESH
         ).wait_recv()
+
+    def wait_sends():
+        while pending:
+            pending.pop().wait_send()
 
     get_kg = pltpu.make_async_copy(kg_in, KG, lsem.at[0])
     get_x = pltpu.make_async_copy(x_in, X, lsem.at[1])
@@ -105,7 +110,7 @@
     def w_arrived(i, dst, cols=whole):
         arrived(WR.at[(*dst, slice(None), cols)], ws.at[i], wr.at[i], to_x(1))
 
-    near = ((1, 15), (3, 1), (2, 14))
+    near = ((1, 15), (3, 1), (2, 14 - 12 * c))
 
     def w_cross(i, j, m, cols=whole):
         w_send(i, (0, j, m), (1, j, m), to_x(3), cols)
@@ -130,7 +135,7 @@
     for i, (j, k) in enumerate(near):
         w_send(i, (0, 0, 0), (0, j, 0), to_z(k))
     w_cross(10, 0, 0)
-    for m in (1, 3, 2):
+    for m in (2, 1, 3):
         w_send(2 + m, (0, 0, 0), (0, 0, m), to_z(16 - 4 * m))
 
     def block(k, other=False):
@@ -264,7 +269,7 @@
         x_send(2, p, U3, SB, 1)
         x_send(1, p, D3, DA, 1)
 
-    ways = ((1, 15), (15, 1), (2, 14))
+    ways = ((2 + 12 * c, 14 - 12 * c), (1, 15), (15, 1))
 
     def owned(p):
         x_arrived(1, p, DB, 0)
@@ -284,7 +289,10 @@
             arrived(QR.at[p, i], qs.at[p, i], qr.at[p, i], to_z(k))
             sums = sums + QR[p, i].astype(F32)
         T[p] = sums
-        for m in (1, 3, 2):
+        far(p)
+
+    def far(p):
+        for m in (2, 1, 3):
             mine = T.at[p, rem(lax.div(z, 4) + m, 4)]
             send(mine, TR.at[p, m - 1], ts.at[p, m - 1], tr.at[p, m - 1], to_z(4 * m))
 
@@ -295,6 +303,43 @@
             sums = sums + TR[p, m - 1]
         wg_out[:, 256 * p : 256 * p + 256] = sums
 
+    def terms_last():
+        out = dot(GT[...].reshape(1024, 1024), H[:, 768:1024])
+        AZ[...] = out.reshape(4, 4, 4, 16, 256)
+        for i, (k, _) in enumerate(ways):
+            QB[i] = AZ[:, :, rem(z + k, 4)].astype(BF16)
+            send(QB.at[i], QC.at[i], qbs.at[i], qbr.at[i], to_z(k))
+
+    left, right = slice(0, 128), slice(128, 256)
+
+    def zx_send(i, value):
+        ZS[i] = value.astype(BF16)
+        send(ZS.at[i], ZR.at[i], zxs.at[i], zxr.at[i], to_x(1 if i % 2 == 0 else 3))
+
+    def zx_arrived(i):
+        arrived(ZR.at[i], zxs.at[i], zxr.at[i], to_x(3 if i % 2 == 0 else 1))
+        return ZR[i].astype(F32)
+
+    def last_near():
+        sums = AZ[:, :, rem(z, 4)]
+        for i, (_, k) in enumerate(ways):
+            arrived(QC.at[i], qbs.at[i], qbr.at[i], to_z(k))
+            sums = sums + QC[i].astype(F32)
+        Y[...] = sums
+        zx_send(0, Y[rem(x + 2, NX), :, :, left])
+        zx_send(1, Y[rem(x + 2, NX), :, :, right])
+        zx_send(2, Y[rem(x + 1, NX), :, :, right])
+        zx_send(3, Y[rem(x + 3, NX), :, :, left])
+
+    def last_relay():
+        zx_send(4, Y[rem(x + 1, NX), :, :, left] + zx_arrived(0))
+        zx_send(5, Y[rem(x + 3, NX), :, :, right] + zx_arrived(1))
+
+    def last_owned():
+        T[3, :, :, left] = Y[x, :, :, left] + zx_arrived(3) + zx_arrived(4)
+        T[3, :, :, right] = Y[x, :, :, right] + zx_arrived(2) + zx_arrived(5)
+        far(3)
+
     def unflip(r, _):
         rows = pl.ds(pl.multiple_of(r * 256, 256), 256)
         G[rows, :] = GT[:, :, rows].reshape(1024, 256).T
@@ -309,6 +354,12 @@
         normed = X[part, :].astype(F32) * inv_c[part, :]
         inner = jnp.sum(gain[...] * GH[part, :] * normed, axis=1, keepdims=True)
         IN[mp, j : j + 1, :] = to_row(inner)
+
+    def gain_terms_last():
+        sums = jnp.sum((W[:, :, 768:1024].astype(F32) * AZ[...].reshape(64, 16, 256)).reshape(1024, 256), axis=0, keepdims=True)
+        sums = sums / gain[:, 768:1024]
+        GX[x, 6:7, :] = sums[:, left]
+        GX[x, 7:8, :] = sums[:, right]
 
     def gain_terms(p):
         for h, kept in enumerate(((V.at[p, 0], F1, S2.at[p, 0], D3), (V.at[p, 1], D1, S2.at[p, 1], F3))):
@@ -322,7 +373,7 @@
             GX[x, b : b + 1, :] = sums / gain[:, cols]
 
     def w_place(i, j, m):
-        there = rem(x + i, NX) * NZ + rem(z + NZ + (0, 1, 2, -1)[j] + 4 * m, NZ)
+        there = rem(x + i, NX) * NZ + rem(z + NZ + (0, 1, 2 - 4 * c, -1)[j] + 4 * m, NZ)
         W[there] = WR[i, j, m]
 
     def column(r, i):
@@ -341,6 +392,7 @@
         w_arrived(6 + i, (0, near[i][0], later))
         w_cross(22 + 4 * i, near[i][0], later, most)
 
+    terms_last()
     terms(0)
     w_relayed(10, 0, 0)
     terms(1)
@@ -348,17 +400,17 @@
     w_relayed(14, pl.ds(1, 3), 0)
     terms(2)
     relay(0)
-    terms(3)
     w_relayed(18, 0, later)
     for i, (j, k) in enumerate(near):
         w_send(34 + i, (across, 0, later), (across, j, later), to_z(k), rest)
     relay(1)
     last_cross(0)
+    last_near()
     relay(2)
     last_cross(1)
     lax.fori_loop(0, 4, unflip, 0)
     owned(0)
-    relay(3)
+    last_relay()
     last_cross(2)
     for j in range(4):
         for m in range(4):
@@ -368,30 +420,30 @@
                     w_place(i, j, m)
     owned(1)
     fourth(0)
+    last_owned()
     w_relay(22, near[0][0], later, most)
     for r in range(4):
         choose(r)
+    w_relay(26, near[1][0], later, most)
+    w_relay(30, near[2][0], later, most)
     owned(2)
     fourth(1)
-    w_relay(26, near[1][0], later, most)
-    w_relay(30, near[2][0], later, most)
     for i, (j, k) in enumerate(near):
         w_arrived(34 + i, (across, j, later), rest)
-    owned(3)
     for i, (j, k) in enumerate(near):
         w_relayed(22 + 4 * i, j, later, most)
     for j in (1, 2, 3):
         for m in (1, 2, 3):
             for i in (1, 2, 3):
                 w_place(i, j, m)
-    for p in range(4):
+    for p in range(3):
         gain_terms(p)
+    gain_terms_last()
     for k in range(1, NX):
         send(GX.at[x], GX.at[x], gxs.at[k], gxr.at[k], to_x(k))
+    backward(0)
     fourth(2)
-    backward(0)
     backward(1)
-    fourth(3)
     backward(2)
     backward(3)
     for j in range(8):
@@ -401,10 +453,12 @@
     for k in range(1, NX):
         arrived(GX.at[rem(x + NX - k, NX)], gxs.at[k], gxr.at[k], to_x(NX - k))
     GZ[z] = GX[0] + GX[1] + GX[2] + GX[3]
-    for k in range(1, NZ):
+    for k in sorted(range(1, NZ), key=lambda k: abs(k - 8)):
         send(GZ.at[z], GZ.at[z], gzs.at[k], gzr.at[k], to_z(k))
     complete(0)
+    complete(3)
     complete(1)
+    wait_sends()
     for k in range(1, 8):
         arrived(IN.at[rem(mp + 8 - k, 8)], ins.at[k], inr.at[k], to_mp(8 - k))
     total = IN[0]
@@ -431,7 +485,6 @@
 
     written = [place(r) for r in range(4)]
     complete(2)
-    complete(3)
     for k in range(1, NZ):
         arrived(GZ.at[rem(z + NZ - k, NZ)], gzs.at[k], gzr.at[k], to_z(NZ - k))
     total = GZ[0]
@@ -440,8 +493,7 @@
     gg_out[...] = total
     for copy in written:
         copy.wait()
-    for copy in pending:
-        copy.wait_send()
+    wait_sends()
 
 
 def deliver(rows_in, wg_in, gg_in, rows_out, wg_out, gg_out, rows, wg, gg, sem):
@@ -502,6 +554,12 @@
         pltpu.VMEM((4, 3, 4, 16, 256), BF16),
         pltpu.VMEM((4, 4, 16, 256), F32),
         pltpu.VMEM((4, 3, 16, 256), F32),
+        pltpu.VMEM((4, 4, 4, 16, 256), F32),
+        pltpu.VMEM((3, 4, 4, 16, 256), BF16),
+        pltpu.VMEM((3, 4, 4, 16, 256), BF16),
+        pltpu.VMEM((4, 4, 16, 256), F32),
+        pltpu.VMEM((6, 4, 16, 128), BF16),
+        pltpu.VMEM((6, 4, 16, 128), BF16),
         dma((6,)), dma((4,)),
         dma((37,)), dma((37,)),
         dma((10,)), dma((10,)),
@@ -512,6 +570,8 @@
         dma((3, 4, 2)), dma((3, 4, 2)),
         dma((4, 3)), dma((4, 3)),
         dma((4, 3)), dma((4, 3)),
+        dma((3,)), dma((3,)),
+        dma((6,)), dma((6,)),
     ]
     row_grads, weight_grad, gain_grad = pl.pallas_call(
         kernel,

time: 81.9 us -> 78.8 us (0.962)
  Pallas kernels: 79.9 us -> 77.3 us
    pallas_call x1, Pallas kernels: 77.5 us -> 74.9 us  [shards(): pl.pallas_call(kernel, out_shape=(jax.ShapeDtypeStruct((1024, 1024), BF16...]
where the time goes in v4:
time: 78.8 us; the launch traced here: 78.6 us
  Pallas kernels  77.3 us (98%)
  between operations  1.29 us (2%)
    pallas_call x1, Pallas kernels, shards(): pl.pallas_call(kernel, out_shape=(jax.ShapeDtypeStruct((1024, 1024), BF16...  74.9 us
    pallas_call x1, Pallas kernels, shards(): pl.pallas_call(deliver, out_shape=(jax.ShapeDtypeStruct((1024, 1024), BF1...  2.45 us

profile of v4, /device:TPU:1, one launch (start us, length us, event | category | flops | bytes accessed | tf_op | source)
XLA Modules:
  0.0 78.6 jit_solution(8138179074559085461)
XLA Ops:
  1.3 74.9 %norm_key_backward.1 = (bf16[1024,1024]{1,0:T(8,128)(2,1)}, f32[16,1024]{1,0:T(8,128)}, f32[8,128]{1,0:T(8,128)}) custom-call(bf16[1024,1024]{1,0:T(8,128)(2,1)} %x_in.1, bf16[1024,128]{1,0:T(8,128)(2,1)} %kg_in.1, bf16[16,1024]{1,0:T(8,128)(2,1)} %w_in.1, f32[1,1024]{1,0:T(1,128)} %bitcast.2, s32[1,1024]{1,0:T(1,128)} %picked_in.1, s32[1]{0:T(128)S(6)} %copy.9.count_in), custom_call_target="tpu_custom_call" | custom-call | flops 6442450944 | bytes 8388608 | tf_op jit(solution)/shard_map/norm_key_backward/pallas_call | solution.py:576
  76.1 2.4 %deliver.1 = (bf16[1024,1024]{1,0:T(8,128)(2,1)}, f32[16,1024]{1,0:T(8,128)}, f32[8,128]{1,0:T(8,128)}) custom-call(bf16[1024,1024]{1,0:T(8,128)(2,1)} %get-tuple-element.9.rows_in, f32[16,1024]{1,0:T(8,128)} %get-tuple-element.10.wg_in, f32[8,128]{1,0:T(8,128)} %get-tuple-element.11.gg_in), custom_call_target="tpu_custom_call" | custom-call | tf_op jit(solution)/shard_map/deliver/pallas_call | solution.py:592

commit v5 on v4

--- a/solution.py
+++ b/solution.py
@@ -31,7 +31,7 @@
     S2, D1, D3, F1, F3, V, U1, U3, R,
     RA, RB, DA, DB, SA, SB, QA, QR, T, TR,
     AZ, QB, QC, Y, ZS, ZR,
-    lsem, osem, ws, wr, ys, yr, sqs, sqr, ins, inr, gxs, gxr, gzs, gzr,
+    hello, hello_far, lsem, osem, ws, wr, ys, yr, sqs, sqr, ins, inr, gxs, gxr, gzs, gzr,
     xs, xr, qs, qr, ts, tr, qbs, qbr, zxs, zxr,
 ):
     dp, mp = lax.axis_index("dp"), lax.axis_index("mp")
@@ -83,7 +83,7 @@
     get_count.start()
 
     barrier = pltpu.get_barrier_semaphore()
-    for k in range(1, NZ):
+    for k in (2, 14, 1, 15):
         pl.semaphore_signal(barrier, inc=1, device_id=to_z(k), device_id_type=MESH)
     for k in range(1, NX):
         pl.semaphore_signal(barrier, inc=1, device_id=to_x(k), device_id_type=MESH)
@@ -99,7 +99,9 @@
 
     lax.fori_loop(0, 8, flip, 0)
     get_w.wait()
-    pl.semaphore_wait(barrier, 7 + NX - 1 + NZ - 1)
+    pl.semaphore_wait(barrier, 7 + NX - 1 + 4)
+    for k in (2, 14):
+        pl.semaphore_signal(hello, inc=1, device_id=to_z(k), device_id_type=MESH)
 
     whole, most, rest = pl.ds(0, 1024), pl.ds(0, 512), pl.ds(512, 512)
     later = pl.ds(1, 3)
@@ -135,8 +137,6 @@
     for i, (j, k) in enumerate(near):
         w_send(i, (0, 0, 0), (0, j, 0), to_z(k))
     w_cross(10, 0, 0)
-    for m in (2, 1, 3):
-        w_send(2 + m, (0, 0, 0), (0, 0, m), to_z(16 - 4 * m))
 
     def block(k, other=False):
         return rem(y + k, NY) * 2 + ((1 - c) if other else c)
@@ -171,6 +171,12 @@
     for k in range(1, 8):
         send(SQ.at[mp], SQ.at[mp], sqs.at[k], sqr.at[k], to_mp(k))
 
+    pl.semaphore_wait(hello, 2)
+    for k in (4, 12):
+        pl.semaphore_signal(hello_far, inc=1, device_id=to_z(k), device_id_type=MESH)
+    for m in (1, 3):
+        w_send(2 + m, (0, 0, 0), (0, 0, m), to_z(16 - 4 * m))
+
     get_picked.wait()
     get_count.wait()
     get_gain.wait()
@@ -184,6 +190,9 @@
         return 0
 
     lax.fori_loop(0, 8, selected, 0)
+
+    pl.semaphore_wait(hello_far, 2)
+    w_send(4, (0, 0, 0), (0, 0, 2), to_z(8))
 
     for i, (j, k) in enumerate(near):
         w_arrived(i, (0, j, 0))
@@ -560,6 +569,8 @@
         pltpu.VMEM((4, 4, 16, 256), F32),
         pltpu.VMEM((6, 4, 16, 128), BF16),
         pltpu.VMEM((6, 4, 16, 128), BF16),
+        pltpu.SemaphoreType.REGULAR,
+        pltpu.SemaphoreType.REGULAR,
         dma((6,)), dma((4,)),
         dma((37,)), dma((37,)),
         dma((10,)), dma((10,)),

time: 78.8 us -> 75.4 us (0.957)
  Pallas kernels: 77.3 us -> 73.9 us
    pallas_call x1, Pallas kernels: 74.9 us -> 71.5 us  [shards(): pl.pallas_call(kernel, out_shape=(jax.ShapeDtypeStruct((1024, 1024), BF16...]
where the time goes in v5:
time: 75.4 us; the launch traced here: 75.2 us
  Pallas kernels  73.9 us (98%)
  between operations  1.29 us (2%)
    pallas_call x1, Pallas kernels, shards(): pl.pallas_call(kernel, out_shape=(jax.ShapeDtypeStruct((1024, 1024), BF16...  71.5 us
    pallas_call x1, Pallas kernels, shards(): pl.pallas_call(deliver, out_shape=(jax.ShapeDtypeStruct((1024, 1024), BF1...  2.45 us

profile of v5, /device:TPU:1, one launch (start us, length us, event | category | flops | bytes accessed | tf_op | source)
XLA Modules:
  0.0 75.2 jit_solution(2166256949091221932)
XLA Ops:
  1.3 71.5 %norm_key_backward.1 = (bf16[1024,1024]{1,0:T(8,128)(2,1)}, f32[16,1024]{1,0:T(8,128)}, f32[8,128]{1,0:T(8,128)}) custom-call(bf16[1024,1024]{1,0:T(8,128)(2,1)} %x_in.1, bf16[1024,128]{1,0:T(8,128)(2,1)} %kg_in.1, bf16[16,1024]{1,0:T(8,128)(2,1)} %w_in.1, f32[1,1024]{1,0:T(1,128)} %bitcast.2, s32[1,1024]{1,0:T(1,128)} %picked_in.1, s32[1]{0:T(128)S(6)} %copy.9.count_in), custom_call_target="tpu_custom_call" | custom-call | flops 6442450944 | bytes 8388608 | tf_op jit(solution)/shard_map/norm_key_backward/pallas_call | solution.py:587
  72.8 2.4 %deliver.1 = (bf16[1024,1024]{1,0:T(8,128)(2,1)}, f32[16,1024]{1,0:T(8,128)}, f32[8,128]{1,0:T(8,128)}) custom-call(bf16[1024,1024]{1,0:T(8,128)(2,1)} %get-tuple-element.9.rows_in, f32[16,1024]{1,0:T(8,128)} %get-tuple-element.10.wg_in, f32[8,128]{1,0:T(8,128)} %get-tuple-element.11.gg_in), custom_call_target="tpu_custom_call" | custom-call | tf_op jit(solution)/shard_map/deliver/pallas_call | solution.py:603
